TPU v7x, 32 devices: a whole 2x2x4 slice. The times are simulated.
32 devices in a mesh: groups: 2 (over x), slab: 16 (over z, y, core).
Axes of the slice: x: 2, y: 2, z: 4, core: 2. Of those that a mesh axis runs over, the one named last changes fastest.
Arguments:
- latent: bfloat16 [64, 32, 2048], P(None, ('groups', 'slab')), parts along dimension 1, may hold values from -6 to 6
- conv1_weight: bfloat16 [27, 64, 64], replicated, may hold values from -0.15625 to 0.15625
- conv2_weight: bfloat16 [27, 64, 64], replicated, may hold values from -0.15625 to 0.15625
- head: bfloat16 [64], replicated, may hold values from -2 to 2
- p_prev: float32 [32, 16, 64, 128], P(('groups', 'slab')), parts along dimension 0, may hold values from -6 to 6
- p_cur: float32 [32, 16, 64, 128], P(('groups', 'slab')), parts along dimension 0, may hold values from -6 to 6
- adjoint: bfloat16 [4, 32, 16, 64, 128], P(None, ('groups', 'slab')), parts along dimension 1, may hold values from -6 to 6
- wavelet: float32 [16, 4], P('groups'), parts along dimension 0, may hold values from -12 to 12
- sources: int32 [16, 3], P('groups'), parts along dimension 0, may hold values from 0 to 127, as said below
- receivers: int32 [16, 3, 128], P('groups'), parts along dimension 0, may hold values from 0 to 127, as said below
Outputs:
- pressure_final: float32 [32, 16, 64, 128], P(('groups', 'slab')), parts along dimension 0
- traces: float32 [16, 4, 128], P('groups'), parts along dimension 0
- gradient: float32 [32, 2048], P(('groups', 'slab')), parts along dimension 0
There are 2 independent parts, one for each index of `groups`. A program takes and returns all parts, laid end to end along the dimension named above; an argument that names none is the same for every part. Nothing has to cross between parts.
Inputs may be any that keep to these rules, and one draw needn't show every extreme that they name: sources[s] is the source cell (depth, row, column) of shot s on the fine grid: depth below 32, row below 64, column below 128. receivers[s, :, k] is the cell (depth, row, column) of receiver k of shot s on the fine grid: depth below 32, row below 64, column below 128.
All inputs are finite; a program needn't handle non-finite values.
Results may differ from a plain program's by a relative error of at most 0.006.
Values may be sent and summed in bfloat16 or wider, within the bound.
A program may use at most 64 MiB of HBM per device.

v0:
```python
import jax
import jax.numpy as jnp
from jax import lax
from jax.sharding import PartitionSpec as P

CY = 32
CX = 64
SHOTS = 8
STEPS = 4


stencil_weights = (-205.0 / 72.0, 8.0 / 5.0, -1.0 / 5.0, 8.0 / 315.0, -1.0 / 560.0)
lowest_speed = 1.5
speed_range = 3.0
courant = 0.088
leak_slope = 0.2


def extended_2(block, sides, width):
    for axis, dim in sides:
        count = lax.axis_size(axis)
        forward = [(i, i + 1) for i in range(count - 1)]
        backward = [(target, source) for source, target in forward]
        low = lax.ppermute(
            lax.slice_in_dim(block, block.shape[dim] - width, None, axis=dim), axis, forward
        )
        high = lax.ppermute(lax.slice_in_dim(block, 0, width, axis=dim), axis, backward)
        block = jnp.concatenate([low, block, high], axis=dim)
    return block


def from_partner(value, axis, apart):
    mask = 2**apart
    pairs = [(source, source ^ mask) for source in range(lax.axis_size(axis))]
    return lax.ppermute(value, axis, pairs)


def for_sending(shard):
    return jax.tree.map(lambda a: a.astype(jnp.bfloat16) if a.dtype == jnp.float32 else a, shard)


def from_behind(value, axis, steps):
    count = lax.axis_size(axis)
    leading, last = (max(0, -steps), min(count, count - steps))
    return lax.ppermute(value, axis, [(source, source + steps) for source in range(leading, last)])


def conv_taps(extended_in, weight):
    planes = extended_in.shape[1] - 2
    cell_count = extended_in.shape[2]
    extended = jnp.pad(extended_in, ((0, 0), (0, 0), (CX + 1, CX + 1)))
    columns = jnp.arange(cell_count) % CX
    accumulated = jnp.zeros((weight.shape[1], planes, cell_count), jnp.float32)
    tap_index = 0
    for depth_off in range(3):
        for row_off in (-1, 0, 1):
            for col_off in (-1, 0, 1):
                begin_at = CX + 1 + row_off * CX + col_off
                piece = extended[
                    :, depth_off : depth_off + planes, begin_at : begin_at + cell_count
                ]
                column_valid = ((columns + col_off >= 0) & (columns + col_off < CX)).astype(
                    extended.dtype
                )
                accumulated = accumulated + jnp.einsum(
                    "oi,izn->ozn",
                    weight[tap_index],
                    piece * column_valid,
                    preferred_element_type=jnp.float32,
                )
                tap_index += 1
    return accumulated


def double_axis(values, axis):
    length = values.shape[axis]
    lower_side = jnp.concatenate(
        [
            lax.slice_in_dim(values, 0, 1, axis=axis),
            lax.slice_in_dim(values, 0, length - 1, axis=axis),
        ],
        axis=axis,
    )
    upper_side = jnp.concatenate(
        [
            lax.slice_in_dim(values, 1, length, axis=axis),
            lax.slice_in_dim(values, length - 1, length, axis=axis),
        ],
        axis=axis,
    )
    even_part = 0.75 * values + 0.25 * lower_side
    odd_part = 0.75 * values + 0.25 * upper_side
    new_shape = list(values.shape)
    new_shape[axis] = 2 * length
    return jnp.stack([even_part, odd_part], axis=axis + 1).reshape(new_shape)


def double_depth(rimmed):
    inner_planes = rimmed.shape[0] - 2
    middle = rimmed[1:-1]
    even_part = 0.75 * middle + 0.25 * rimmed[:-2]
    odd_part = 0.75 * middle + 0.25 * rimmed[2:]
    return jnp.stack([even_part, odd_part], axis=1).reshape((2 * inner_planes,) + rimmed.shape[1:])


def upsample_slab(rimmed):
    deeper = double_depth(rimmed).reshape(2 * (rimmed.shape[0] - 2), CY, CX)
    return double_axis(double_axis(deeper, 1), 2)


def stencil(extended):
    depth_total = extended.shape[0] - 8
    row_total = extended.shape[1]
    col_total = extended.shape[2]
    padded = jnp.pad(extended, ((0, 0), (4, 4), (4, 4)))

    def window(depth_at, row_at, col_at):
        return padded[
            depth_at : depth_at + depth_total,
            row_at : row_at + row_total,
            col_at : col_at + col_total,
        ]

    accumulated = 3.0 * stencil_weights[0] * window(4, 4, 4)
    for reach in range(1, 5):
        near_sum = window(4 - reach, 4, 4) + window(4 + reach, 4, 4)
        near_sum = near_sum + window(4, 4 - reach, 4) + window(4, 4 + reach, 4)
        near_sum = near_sum + window(4, 4, 4 - reach) + window(4, 4, 4 + reach)
        accumulated = accumulated + stencil_weights[reach] * near_sum
    return accumulated


def body(
    latent, conv1_weight, conv2_weight, head, p_prev, p_cur, adjoint, wavelet, sources, receivers
):
    position = lax.axis_index("slab")
    devices = lax.axis_size("slab")
    my_shot = position % SHOTS
    slab_index = position // SHOTS
    slab_total = devices // SHOTS
    group_bits = SHOTS.bit_length() - 1
    latent_wide = extended_2(latent, (("slab", 1),), 1)
    hidden = jax.nn.leaky_relu(conv_taps(latent_wide, conv1_weight), leak_slope).astype(
        jnp.bfloat16
    )
    hidden_wide = extended_2(hidden, (("slab", 1),), 1)
    second = jax.nn.leaky_relu(conv_taps(hidden_wide, conv2_weight), leak_slope)
    logits = jnp.einsum(
        "c,czn->zn", head.astype(jnp.float32), second, precision=lax.Precision.HIGHEST
    )
    velocity = (lowest_speed + speed_range * jax.nn.sigmoid(logits)).astype(jnp.bfloat16)
    planes = velocity.shape[0]
    slab_planes = planes * SHOTS
    rimmed = extended_2(velocity, (("slab", 0),), 1)
    rimmed = jnp.concatenate(
        [
            jnp.where(position == 0, velocity, rimmed[:1]),
            rimmed[1:-1],
            jnp.where(position == devices - 1, velocity, rimmed[-1:]),
        ],
        axis=0,
    )
    tile_doubled = double_depth(rimmed.astype(jnp.float32))
    bit_order = list(range(group_bits))
    blocks = tile_doubled[None]
    for bit_index in bit_order:
        partner = from_partner(blocks, "slab", bit_index)
        upper_bit = my_shot // (1 << bit_index) % 2 == 1
        blocks = jnp.where(
            upper_bit,
            jnp.concatenate([partner, blocks], axis=0),
            jnp.concatenate([blocks, partner], axis=0),
        )
    placed = []
    for shot_number in range(SHOTS):
        list_index = 0
        for section_number in range(group_bits):
            list_index = list_index + (
                (shot_number >> bit_order[section_number] & 1) << section_number
            )
        placed.append(blocks[list_index])
    deeper = jnp.concatenate(placed, axis=0).reshape(2 * slab_planes, CY, CX)
    fine_speed = double_axis(double_axis(deeper, 1), 2)
    courant_sq = (courant * fine_speed) ** 2
    previous = p_prev[0]
    current = p_cur[0]
    fine_planes = current.shape[0]
    offset = slab_index * fine_planes
    source = lax.dynamic_index_in_dim(sources, my_shot, 0, keepdims=False)
    station = lax.dynamic_index_in_dim(receivers, my_shot, 0, keepdims=False)
    pulses = lax.dynamic_index_in_dim(wavelet, my_shot, 0, keepdims=False)
    source_depth = source[0] - offset
    source_inside = (source_depth >= 0) & (source_depth < fine_planes)
    source_depth = jnp.clip(source_depth, 0, fine_planes - 1)
    station_depth = station[0] - offset
    station_inside = (station_depth >= 0) & (station_depth < fine_planes)
    station_depth = jnp.clip(station_depth, 0, fine_planes - 1)
    correlation = jnp.zeros(current.shape, jnp.float32)
    samples_list = []
    for step_index in range(STEPS):
        rim_below = from_behind(for_sending(current[-4:]), "slab", SHOTS)
        rim_above = from_behind(for_sending(current[:4]), "slab", -SHOTS)
        laplace_term = stencil(jnp.concatenate([rim_below, current, rim_above], axis=0))
        correlation = correlation + adjoint[step_index, 0].astype(jnp.float32) * laplace_term
        advanced = 2.0 * current - previous + courant_sq * laplace_term
        advanced = advanced.at[source_depth, source[1], source[2]].add(
            jnp.where(source_inside, pulses[step_index], 0.0)
        )
        samples_list.append(
            jnp.where(station_inside, advanced[station_depth, station[1], station[2]], 0.0)
        )
        previous, current = (current, advanced)
    record = jnp.stack(samples_list)
    own_traces = jnp.where((jnp.arange(SHOTS) == my_shot)[:, None, None], record[None], 0.0)
    traces = lax.psum(own_traces, "slab")
    fine_gradient = 2.0 * courant * courant * fine_speed * correlation
    shape_holder = jnp.zeros((slab_planes + 2, velocity.shape[1]), jnp.float32)
    unused, pullback = jax.vjp(upsample_slab, shape_holder)
    grad_rim = pullback(fine_gradient)[0]
    first_slab = slab_index == 0
    last_slab = slab_index == slab_total - 1
    folded = jnp.concatenate(
        [
            jnp.where(first_slab, 0.0, grad_rim[:1]),
            grad_rim[1:2] + jnp.where(first_slab, grad_rim[:1], 0.0),
            grad_rim[2:-2],
            grad_rim[-2:-1] + jnp.where(last_slab, grad_rim[-1:], 0.0),
            jnp.where(last_slab, 0.0, grad_rim[-1:]),
        ],
        axis=0,
    )
    from_lower = from_behind(folded[-1:], "slab", SHOTS)
    from_upper = from_behind(folded[:1], "slab", -SHOTS)
    inner = folded[1:-1]
    inner = jnp.concatenate([inner[:1] + from_lower, inner[1:-1], inner[-1:] + from_upper], axis=0)
    blocks = inner.reshape(SHOTS, planes, inner.shape[1])
    for bit_index in reversed(range(group_bits)):
        halfway = blocks.shape[0] // 2
        upper_bit = my_shot // (1 << bit_index) % 2 == 1
        retained = jnp.where(upper_bit, blocks[halfway:], blocks[:halfway])
        outgoing = jnp.where(upper_bit, blocks[:halfway], blocks[halfway:])
        blocks = retained + from_partner(outgoing, "slab", bit_index)
    gradient = blocks[0]
    return (current[None], traces, gradient)


def solution(mesh):
    in_specs = (
        P(None, ("groups", "slab"), None),
        P(),
        P(),
        P(),
        P(("groups", "slab"), None, None, None),
        P(("groups", "slab"), None, None, None),
        P(None, ("groups", "slab"), None, None, None),
        P("groups", None),
        P("groups", None),
        P("groups", None, None),
    )
    out_specs = (
        P(("groups", "slab"), None, None, None),
        P("groups", None, None),
        P(("groups", "slab"), None),
    )
    return jax.shard_map(body, mesh=mesh, in_specs=in_specs, out_specs=out_specs, check_vma=False)
```

profile of v0, /device:TPU:0, one launch (start us, length us, event | category | flops | bytes accessed | tf_op | source)
XLA Modules:
  0.0 228.8 jit_solution(11264955654170186735)
XLA Ops:
  0.7 1.4 collective-permute-start.1
  2.1 3.1 %collective-permute-start = (bf16[64,1,2048]{2,0,1:T(8,128)(2,1)}, bf16[64,1,2048]{2,0,1:T(8,128)(2,1)S(1)}, u32[]{:S(2)}, u32[]{:S(2)}) collective-permute-start(bf16[64,1,2048]{2,0,1:T(8,128)(2,1)} %param.18), channel_id=1, source_target_pairs={{0,1},{1,2},{2,3},{3,4},{4,5},{5,6},{6,7},{7,8},{8,9},{9,10},{10,1... | collective-permute-start | bytes 786440 | tf_op jit(solution)/shard_map/ppermute | solution.py:24
  5.2 1.1 convert.20
  6.5 1.3 fusion.32
  15.2 1.3 collective-permute-start.3
  16.5 9.2 %collective-permute-start.2 = (bf16[64,1,2048]{2,0,1:T(8,128)(2,1)S(1)}, bf16[64,1,2048]{2,0,1:T(8,128)(2,1)S(1)}, u32[]{:S(2)}, u32[]{:S(2)}) collective-permute-start(bf16[64,1,2048]{2,0,1:T(8,128)(2,1)S(1)} %bitcast.577), channel_id=1, source_target_pairs={{0,1},{1,2},{2,3},{3,4},{4,5},{5,6},{6,7},{7,8},{8,9},{9,10},{10,1... | collective-permute-start | bytes 786440 | tf_op jit(solution)/shard_map/ppermute | solution.py:24
  25.7 5.7 %collective-permute-start.9 = (bf16[4,64,128]{2,1,0:T(8,128)(2,1)S(1)}, bf16[4,64,128]{2,1,0:T(8,128)(2,1)S(1)}, u32[]{:S(2)}, u32[]{:S(2)}) collective-permute-start(bf16[4,64,128]{2,1,0:T(8,128)(2,1)S(1)} %get-tuple-element.81), channel_id=1, source_target_pairs={{0,8},{1,9},{2,10},{3,11},{4,12},{5,13},{6,14},{7,15},{16,24},{17,... | collective-permute-start | bytes 196616 | tf_op jit(solution)/shard_map/ppermute | solution.py:45
  31.4 1.3 collective-permute-start.10
  32.8 0.6 fusion.496
  41.6 1.3 collective-permute-start.5
  42.9 3.6 %collective-permute-start.4 = (bf16[1,2048]{1,0:T(2,128)(2,1)S(1)}, bf16[1,2048]{1,0:T(2,128)(2,1)S(1)}, u32[]{:S(2)}, u32[]{:S(2)}) collective-permute-start(bf16[1,2048]{1,0:T(2,128)(2,1)S(1)} %convert_element_type.266), channel_id=1, source_target_pairs={{0,1},{1,2},{2,3},{3,4},{4,5},{5,6},{6,7},{7,8},{8,9},{9,10},{10,1... | collective-permute-start | bytes 12296 | tf_op jit(solution)/shard_map/ppermute | solution.py:24
  46.7 0.5 collective-permute-done.4
  47.4 1.8 collective-permute-start.6
  54.2 2.4 %collective-permute-start.7 = (f32[2,2,2048]{2,1,0:T(2,128)S(1)}, f32[2,2,2048]{2,1,0:T(2,128)S(1)}, u32[]{:S(2)}, u32[]{:S(2)}) collective-permute-start(f32[2,2,2048]{2,1,0:T(2,128)S(1)} %maximum_select_fusion.2), channel_id=1, source_target_pairs={{0,2},{1,3},{2,0},{3,1},{4,6},{5,7},{6,4},{7,5},{8,10},{9,11},{10,... | collective-permute-start | bytes 98312 | tf_op jit(solution)/shard_map/ppermute | solution.py:35
  56.7 0.7 and_reduce_fusion
  60.1 2.2 collective-permute-start.8
  62.3 0.5 select_maximum_fusion.6
  62.8 1.7 collective-permute-done.8
  66.9 1.1 slice_bitcast_fusion.1
  68.0 0.9 fusion.490
  69.2 1.3 copy.54
  71.1 1.1 copy.55
  72.2 1.7 fusion.155
  73.9 1.2 fusion.33
  75.1 1.9 copy.58
  77.0 1.6 copy.59
  78.6 4.4 %fusion.164 = (f32[16,64,128]{2,1,0:T(8,128)S(1)}, f32[16,64,128]{2,1,0:T(8,128)}) fusion(f32[1,16,64,128]{3,2,1,0:T(8,128)} %param.22, f32[16,64,128]{2,1,0:T(8,128)S(1)} %copy.59, f32[1,16,64,128]{3,2,1,0:T(8,128)S(1)} %copy-done.2, f32[24,72,136]{2,1,0:T(8,128)S(1)} %select_maximum_fusion.6, f32[4,64,128]{2,1,0:T(8,128)} %copy-done.11, ...), kind=kLoop, calls=%fused_computation.321 | loop fusion | flops 5373952 | bytes 11796480 | tf_op jit(solution)/shard_map/add | solution.py:205
  83.0 0.6 dynamic-slice.33
  85.7 5.2 %collective-permute-start.11 = (bf16[4,64,128]{2,1,0:T(8,128)(2,1)S(1)}, bf16[4,64,128]{2,1,0:T(8,128)(2,1)S(1)}, u32[]{:S(2)}, u32[]{:S(2)}) collective-permute-start(bf16[4,64,128]{2,1,0:T(8,128)(2,1)S(1)} %get-tuple-element.79), channel_id=1, source_target_pairs={{0,8},{1,9},{2,10},{3,11},{4,12},{5,13},{6,14},{7,15},{16,24},{17,... | collective-permute-start | bytes 196616 | tf_op jit(solution)/shard_map/ppermute | solution.py:45
  90.8 1.3 collective-permute-start.12
  92.1 0.6 collective-permute-done.11
  92.7 5.2 %collective-permute-done.12 = bf16[4,64,128]{2,1,0:T(8,128)(2,1)S(1)} collective-permute-done((bf16[4,64,128]{2,1,0:T(8,128)(2,1)S(1)}, bf16[4,64,128]{2,1,0:T(8,128)(2,1)S(1)}, u32[]{:S(2)}, u32[]{:S(2)}) %collective-permute-start.12) | collective-permute-done | bytes 65568 | tf_op jit(solution)/shard_map/ppermute | solution.py:45
  97.9 0.6 copy-done.13
  99.1 4.2 %multiply_add_fusion.2 = (f32[16,64,128]{2,1,0:T(8,128)S(1)}, f32[16,64,128]{2,1,0:T(8,128)}) fusion(f32[16,64,128]{2,1,0:T(8,128)} %copy-done.3, f32[16,64,128]{2,1,0:T(8,128)S(1)} %scatter-add.14, f32[1,16,64,128]{3,2,1,0:T(8,128)S(1)} %copy-done.2, f32[24,72,136]{2,1,0:T(8,128)S(1)} %select_maximum_fusion.4, f32[4,64,128]{2,1,0:T(8,128)} %copy-done.13, ...), kind=kLoop, calls=%fused_computation.326 | loop fusion | flops 5373952 | bytes 11272192 | tf_op jit(solution)/shard_map/add | solution.py:205
  103.3 0.7 dynamic-slice.34
  106.1 1.6 collective-permute-start.13
  107.7 1.5 collective-permute-start.14
  109.2 0.7 fusion.483
  110.0 1.5 gather_fusion
  111.5 3.3 %collective-permute-done.14 = bf16[4,64,128]{2,1,0:T(8,128)(2,1)S(1)} collective-permute-done((bf16[4,64,128]{2,1,0:T(8,128)(2,1)S(1)}, bf16[4,64,128]{2,1,0:T(8,128)(2,1)S(1)}, u32[]{:S(2)}, u32[]{:S(2)}) %collective-permute-start.14) | collective-permute-done | bytes 65568 | tf_op jit(solution)/shard_map/ppermute | solution.py:45
  114.8 0.6 copy-done.12
  116.0 4.2 %multiply_add_fusion.1 = (f32[16,64,128]{2,1,0:T(8,128)S(1)}, f32[16,64,128]{2,1,0:T(8,128)}) fusion(f32[16,64,128]{2,1,0:T(8,128)} %copy-done.3, f32[16,64,128]{2,1,0:T(8,128)S(1)} %scatter-add.14, f32[16,64,128]{2,1,0:T(8,128)S(1)} %scatter-add.15, f32[24,72,136]{2,1,0:T(8,128)S(1)} %select_maximum_fusion.2, f32[4,64,128]{2,1,0:T(8,128)} %copy-done.12, ...), kind=kLoop, calls=%fused_computation.325 | loop fusion | flops 5373952 | bytes 11272192 | tf_op jit(solution)/shard_map/add | solution.py:205
  120.2 0.7 dynamic-slice.35
  123.0 2.2 collective-permute-start.15
  125.2 1.3 collective-permute-start.16
  126.5 0.7 bitcast_select_fusion.3
  127.2 2.0 copy.63
  129.2 2.4 %copy.64 = f32[16,64,128]{2,1,0:T(8,128)} copy(f32[16,64,128]{1,0,2:T(8,128)} %bitcast.569) | data formatting | bytes 1048576 | tf_op jit(solution)/shard_map/mul | solution.py:216
  131.6 1.5 gather_fusion.1
  133.1 1.5 gather_fusion.2
  134.7 0.5 select_maximum_fusion
  136.0 3.4 %fusion.158 = (f32[16,64,128]{2,1,0:T(8,128)}, f32[16,64,128]{2,1,0:T(8,128)S(1)}) fusion(f32[16,64,128]{2,1,0:T(8,128)S(1)} %copy-done.10, f32[16,64,128]{2,1,0:T(8,128)S(1)} %copy-done.9, f32[16,64,128]{2,1,0:T(8,128)S(1)} %copy-done.8, f32[16,64,128]{2,1,0:T(8,128)S(1)} %copy-done.7, bf16[4,1,16,64,128]{4,3,2,1,0:T(8,128)(2,1)S(1)} %copy-done.14, ...), kind=kLoop, calls=%fused_computation.310 | loop fusion | flops 6422528 | bytes 13369344 | tf_op jit(solution)/shard_map/mul | solution.py:216
  139.6 0.6 dynamic-slice.36
  142.2 1.5 gather_fusion.3
  143.7 1.5 copy.65
  148.5 5.4 %collective-permute-start.18 = (f32[1,2048]{1,0:T(1,128)S(1)}, f32[1,2048]{1,0:T(1,128)S(1)}, u32[]{:S(2)}, u32[]{:S(2)}) collective-permute-start(f32[1,2048]{1,0:T(1,128)S(1)} %get-tuple-element.91), channel_id=1, source_target_pairs={{0,8},{1,9},{2,10},{3,11},{4,12},{5,13},{6,14},{7,15},{16,24},{17,... | collective-permute-start | bytes 24584 | tf_op jit(solution)/shard_map/ppermute | solution.py:45
  153.9 1.3 collective-permute-start.17
  155.3 5.1 %collective-permute-done.17 = f32[1,2048]{1,0:T(1,128)S(1)} collective-permute-done((f32[1,2048]{1,0:T(1,128)S(1)}, f32[1,2048]{1,0:T(1,128)S(1)}, u32[]{:S(2)}, u32[]{:S(2)}) %collective-permute-start.17) | collective-permute-done | bytes 8224 | tf_op jit(solution)/shard_map/ppermute | solution.py:45
  160.5 2.1 collective-permute-start.19
  162.6 1.9 collective-permute-done.19
  164.5 1.8 collective-permute-start.20
  166.4 2.0 collective-permute-done.20
  168.4 59.7 %psum.7 = f32[8,4,128]{2,1,0:T(4,128)} all-reduce(f32[8,4,128]{2,1,0:T(4,128)S(1)} %broadcast_select_fusion.9), channel_id=1, replica_groups=mesh['groups'=2,'slab'=16] {'slab'}, use_global_device_ids=true, to_apply=%region_1.2 | all-reduce | flops 4096 | bytes 32768 | tf_op jit(solution)/shard_map/psum | solution.py:215
  228.1 0.6 fusion.446
  (223 shorter events, 25.7 us)
Async XLA Ops:
  0.6 32.1 %copy-start = (f32[8,4]{0,1:T(4,128)S(1)}, f32[8,4]{0,1:T(4,128)}, u32[]{:S(2)}) copy-start(f32[8,4]{0,1:T(4,128)} %param.25) | copy-start | bytes 388
  0.6 7.1 %copy-start.17 = (bf16[27,64,64]{2,1,0:T(8,128)(2,1)S(1)}, bf16[27,64,64]{2,1,0:T(8,128)(2,1)}, u32[]{:S(2)}) copy-start(bf16[27,64,64]{2,1,0:T(8,128)(2,1)} %param.19) | copy-start | bytes 663556
  0.7 5.6 %collective-permute-start.1 = (bf16[64,1,2048]{2,0,1:T(8,128)(2,1)}, bf16[64,1,2048]{2,0,1:T(8,128)(2,1)S(1)}, u32[]{:S(2)}, u32[]{:S(2)}) collective-permute-start(bf16[64,1,2048]{2,0,1:T(8,128)(2,1)} %param.18), channel_id=1, source_target_pairs={{1,0},{2,1},{3,2},{4,3},{5,4},{6,5},{7,6},{8,7},{9,8},{10,9},{11,1... | collective-permute-start | bytes 786440 | tf_op jit(solution)/shard_map/ppermute | solution.py:27
  2.1 4.4 %collective-permute-start = (bf16[64,1,2048]{2,0,1:T(8,128)(2,1)}, bf16[64,1,2048]{2,0,1:T(8,128)(2,1)S(1)}, u32[]{:S(2)}, u32[]{:S(2)}) collective-permute-start(bf16[64,1,2048]{2,0,1:T(8,128)(2,1)} %param.18), channel_id=1, source_target_pairs={{0,1},{1,2},{2,3},{3,4},{4,5},{5,6},{6,7},{7,8},{8,9},{9,10},{10,1... | collective-permute-start | bytes 786440 | tf_op jit(solution)/shard_map/ppermute | solution.py:24
  11.8 1.0 copy-start.15
  14.9 19.0 %copy-start.16 = (bf16[27,64,64]{2,1,0:T(8,128)(2,1)S(1)}, bf16[27,64,64]{2,1,0:T(8,128)(2,1)}, u32[]{:S(2)}) copy-start(bf16[27,64,64]{2,1,0:T(8,128)(2,1)} %param.20) | copy-start | bytes 663556
  15.2 18.2 %collective-permute-start.3 = (bf16[64,1,2048]{2,0,1:T(8,128)(2,1)S(1)}, bf16[64,1,2048]{2,0,1:T(8,128)(2,1)S(1)}, u32[]{:S(2)}, u32[]{:S(2)}) collective-permute-start(bf16[64,1,2048]{2,0,1:T(8,128)(2,1)S(1)} %bitcast.576), channel_id=1, source_target_pairs={{1,0},{2,1},{3,2},{4,3},{5,4},{6,5},{7,6},{8,7},{9,8},{10,9},{11,1... | collective-permute-start | bytes 786440 | tf_op jit(solution)/shard_map/ppermute | solution.py:27
  16.5 16.9 %collective-permute-start.2 = (bf16[64,1,2048]{2,0,1:T(8,128)(2,1)S(1)}, bf16[64,1,2048]{2,0,1:T(8,128)(2,1)S(1)}, u32[]{:S(2)}, u32[]{:S(2)}) collective-permute-start(bf16[64,1,2048]{2,0,1:T(8,128)(2,1)S(1)} %bitcast.577), channel_id=1, source_target_pairs={{0,1},{1,2},{2,3},{3,4},{4,5},{5,6},{6,7},{7,8},{8,9},{9,10},{10,1... | collective-permute-start | bytes 786440 | tf_op jit(solution)/shard_map/ppermute | solution.py:24
  25.7 34.2 %collective-permute-start.9 = (bf16[4,64,128]{2,1,0:T(8,128)(2,1)S(1)}, bf16[4,64,128]{2,1,0:T(8,128)(2,1)S(1)}, u32[]{:S(2)}, u32[]{:S(2)}) collective-permute-start(bf16[4,64,128]{2,1,0:T(8,128)(2,1)S(1)} %get-tuple-element.81), channel_id=1, source_target_pairs={{0,8},{1,9},{2,10},{3,11},{4,12},{5,13},{6,14},{7,15},{16,24},{17,... | collective-permute-start | bytes 196616 | tf_op jit(solution)/shard_map/ppermute | solution.py:45
  31.4 28.6 %collective-permute-start.10 = (bf16[4,64,128]{2,1,0:T(8,128)(2,1)S(1)}, bf16[4,64,128]{2,1,0:T(8,128)(2,1)S(1)}, u32[]{:S(2)}, u32[]{:S(2)}) collective-permute-start(bf16[4,64,128]{2,1,0:T(8,128)(2,1)S(1)} %get-tuple-element.82), channel_id=1, source_target_pairs={{8,0},{9,1},{10,2},{11,3},{12,4},{13,5},{14,6},{15,7},{24,16},{25,... | collective-permute-start | bytes 196616 | tf_op jit(solution)/shard_map/ppermute | solution.py:45
  40.4 0.9 copy-start.19
  40.7 5.9 %copy-start.18 = (s32[8,3]{0,1:T(4,128)S(1)}, s32[8,3]{0,1:T(4,128)}, u32[]{:S(2)}) copy-start(s32[8,3]{0,1:T(4,128)} %param.26) | copy-start | bytes 292
  40.7 16.0 %copy-start.21 = (s32[3]{0:T(128)S(1)}, s32[3]{0:T(128)}, u32[]{:S(2)}) copy-start(s32[3]{0:T(128)} %constant.246.clone.1) | copy-start | bytes 40
  40.7 21.6 %copy-start.2 = (f32[1,16,64,128]{3,2,1,0:T(8,128)S(1)}, f32[1,16,64,128]{3,2,1,0:T(8,128)}, u32[]{:S(2)}) copy-start(f32[1,16,64,128]{3,2,1,0:T(8,128)} %param.23) | copy-start | bytes 1572868
  41.6 5.0 %collective-permute-start.5 = (bf16[1,2048]{1,0:T(2,128)(2,1)S(1)}, bf16[1,2048]{1,0:T(2,128)(2,1)S(1)}, u32[]{:S(2)}, u32[]{:S(2)}) collective-permute-start(bf16[1,2048]{1,0:T(2,128)(2,1)S(1)} %convert_element_type.266), channel_id=1, source_target_pairs={{1,0},{2,1},{3,2},{4,3},{5,4},{6,5},{7,6},{8,7},{9,8},{10,9},{11,1... | collective-permute-start | bytes 12296 | tf_op jit(solution)/shard_map/ppermute | solution.py:27
  42.9 4.3 %collective-permute-start.4 = (bf16[1,2048]{1,0:T(2,128)(2,1)S(1)}, bf16[1,2048]{1,0:T(2,128)(2,1)S(1)}, u32[]{:S(2)}, u32[]{:S(2)}) collective-permute-start(bf16[1,2048]{1,0:T(2,128)(2,1)S(1)} %convert_element_type.266), channel_id=1, source_target_pairs={{0,1},{1,2},{2,3},{3,4},{4,5},{5,6},{6,7},{7,8},{8,9},{9,10},{10,1... | collective-permute-start | bytes 12296 | tf_op jit(solution)/shard_map/ppermute | solution.py:24
  47.4 6.8 %collective-permute-start.6 = (f32[1,2,2048]{2,1,0:T(2,128)S(1)}, f32[1,2,2048]{2,1,0:T(2,128)S(1)}, u32[]{:S(2)}, u32[]{:S(2)}) collective-permute-start(f32[1,2,2048]{2,1,0:T(2,128)S(1)} %pad_maximum_fusion.12), channel_id=1, source_target_pairs={{0,1},{1,0},{2,3},{3,2},{4,5},{5,4},{6,7},{7,6},{8,9},{9,8},{10,11... | collective-permute-start | bytes 49160 | tf_op jit(solution)/shard_map/ppermute | solution.py:35
  54.2 5.8 %collective-permute-start.7 = (f32[2,2,2048]{2,1,0:T(2,128)S(1)}, f32[2,2,2048]{2,1,0:T(2,128)S(1)}, u32[]{:S(2)}, u32[]{:S(2)}) collective-permute-start(f32[2,2,2048]{2,1,0:T(2,128)S(1)} %maximum_select_fusion.2), channel_id=1, source_target_pairs={{0,2},{1,3},{2,0},{3,1},{4,6},{5,7},{6,4},{7,5},{8,10},{9,11},{10,... | collective-permute-start | bytes 98312 | tf_op jit(solution)/shard_map/ppermute | solution.py:35
  60.0 5.3 %copy-start.11 = (f32[4,64,128]{2,1,0:T(8,128)}, f32[4,64,128]{2,1,0:T(8,128)S(1)}, u32[]{:S(2)}) copy-start(f32[4,64,128]{2,1,0:T(8,128)S(1)} %convert_element_type.271) | copy-start | bytes 393220
  60.1 4.5 %collective-permute-start.8 = (f32[4,2,2048]{2,1,0:T(2,128)S(1)}, f32[4,2,2048]{2,1,0:T(2,128)S(1)}, u32[]{:S(2)}, u32[]{:S(2)}) collective-permute-start(f32[4,2,2048]{2,1,0:T(2,128)S(1)} %maximum_select_fusion.1), channel_id=1, source_target_pairs={{0,4},{1,5},{2,6},{3,7},{4,0},{5,1},{6,2},{7,3},{8,12},{9,13},{10,... | collective-permute-start | bytes 196616 | tf_op jit(solution)/shard_map/ppermute | solution.py:35
  78.6 4.4 %copy-start.3 = (f32[16,64,128]{2,1,0:T(8,128)}, f32[16,64,128]{2,1,0:T(8,128)S(1)}, u32[]{:S(2)}) copy-start(f32[16,64,128]{2,1,0:T(8,128)S(1)} %copy.59) | copy-start | bytes 1572868
  85.7 7.1 %collective-permute-start.11 = (bf16[4,64,128]{2,1,0:T(8,128)(2,1)S(1)}, bf16[4,64,128]{2,1,0:T(8,128)(2,1)S(1)}, u32[]{:S(2)}, u32[]{:S(2)}) collective-permute-start(bf16[4,64,128]{2,1,0:T(8,128)(2,1)S(1)} %get-tuple-element.79), channel_id=1, source_target_pairs={{0,8},{1,9},{2,10},{3,11},{4,12},{5,13},{6,14},{7,15},{16,24},{17,... | collective-permute-start | bytes 196616 | tf_op jit(solution)/shard_map/ppermute | solution.py:45
  90.8 7.1 %collective-permute-start.12 = (bf16[4,64,128]{2,1,0:T(8,128)(2,1)S(1)}, bf16[4,64,128]{2,1,0:T(8,128)(2,1)S(1)}, u32[]{:S(2)}, u32[]{:S(2)}) collective-permute-start(bf16[4,64,128]{2,1,0:T(8,128)(2,1)S(1)} %get-tuple-element.80), channel_id=1, source_target_pairs={{8,0},{9,1},{10,2},{11,3},{12,4},{13,5},{14,6},{15,7},{24,16},{25,... | collective-permute-start | bytes 196616 | tf_op jit(solution)/shard_map/ppermute | solution.py:45
  97.9 0.7 copy-start.13
  106.1 5.3 %collective-permute-start.13 = (bf16[4,64,128]{2,1,0:T(8,128)(2,1)S(1)}, bf16[4,64,128]{2,1,0:T(8,128)(2,1)S(1)}, u32[]{:S(2)}, u32[]{:S(2)}) collective-permute-start(bf16[4,64,128]{2,1,0:T(8,128)(2,1)S(1)} %get-tuple-element.77), channel_id=1, source_target_pairs={{0,8},{1,9},{2,10},{3,11},{4,12},{5,13},{6,14},{7,15},{16,24},{17,... | collective-permute-start | bytes 196616 | tf_op jit(solution)/shard_map/ppermute | solution.py:45
  107.7 7.1 %collective-permute-start.14 = (bf16[4,64,128]{2,1,0:T(8,128)(2,1)S(1)}, bf16[4,64,128]{2,1,0:T(8,128)(2,1)S(1)}, u32[]{:S(2)}, u32[]{:S(2)}) collective-permute-start(bf16[4,64,128]{2,1,0:T(8,128)(2,1)S(1)} %get-tuple-element.78), channel_id=1, source_target_pairs={{8,0},{9,1},{10,2},{11,3},{12,4},{13,5},{14,6},{15,7},{24,16},{25,... | collective-permute-start | bytes 196616 | tf_op jit(solution)/shard_map/ppermute | solution.py:45
  114.8 0.7 copy-start.12
  120.1 7.1 %copy-start.5 = (f32[16,64,64,2]{2,0,1,3:T(8,128)S(1)}, f32[16,64,64,2]{2,0,1,3:T(8,128)}, u32[]{:S(2)}) copy-start(f32[16,64,64,2]{2,0,1,3:T(8,128)} %get-tuple-element.63) | copy-start | bytes 1572868
  123.0 11.6 %collective-permute-start.15 = (bf16[4,64,128]{2,1,0:T(8,128)(2,1)S(1)}, bf16[4,64,128]{2,1,0:T(8,128)(2,1)S(1)}, u32[]{:S(2)}, u32[]{:S(2)}) collective-permute-start(bf16[4,64,128]{2,1,0:T(8,128)(2,1)S(1)} %get-tuple-element.75), channel_id=1, source_target_pairs={{0,8},{1,9},{2,10},{3,11},{4,12},{5,13},{6,14},{7,15},{16,24},{17,... | collective-permute-start | bytes 196616 | tf_op jit(solution)/shard_map/ppermute | solution.py:45
  125.2 9.4 %collective-permute-start.16 = (bf16[4,64,128]{2,1,0:T(8,128)(2,1)S(1)}, bf16[4,64,128]{2,1,0:T(8,128)(2,1)S(1)}, u32[]{:S(2)}, u32[]{:S(2)}) collective-permute-start(bf16[4,64,128]{2,1,0:T(8,128)(2,1)S(1)} %get-tuple-element.76), channel_id=1, source_target_pairs={{8,0},{9,1},{10,2},{11,3},{12,4},{13,5},{14,6},{15,7},{24,16},{25,... | collective-permute-start | bytes 196616 | tf_op jit(solution)/shard_map/ppermute | solution.py:45
  133.1 2.1 copy-start.7
  133.1 2.1 copy-start.8
  133.1 2.1 copy-start.9
  134.6 1.0 copy-start.10
  134.6 1.4 copy-start.14
  136.0 3.4 %copy-start.4 = (f32[16,64,128]{2,1,0:T(8,128)S(1)}, f32[16,64,128]{2,1,0:T(8,128)}, u32[]{:S(2)}) copy-start(f32[16,64,128]{2,1,0:T(8,128)} %copy-done.3) | copy-start | bytes 1572868
  142.2 3.1 %copy-start.6 = (f32[16,64,128]{2,1,0:T(8,128)}, f32[16,64,128]{2,1,0:T(8,128)S(1)}, u32[]{:S(2)}) copy-start(f32[16,64,128]{2,1,0:T(8,128)S(1)} %scatter-add.19) | copy-start | bytes 1572868
  146.1 0.7 copy-start.22
  147.1 0.7 copy-start.20
  147.4 81.3 %copy-start.1 = (f32[8,4]{0,1:T(4,128)S(1)}, f32[8,4]{0,1:T(4,128)}, u32[]{:S(2)}) copy-start(f32[8,4]{0,1:T(4,128)} %param.25) | copy-start | bytes 388
  148.5 6.8 %collective-permute-start.18 = (f32[1,2048]{1,0:T(1,128)S(1)}, f32[1,2048]{1,0:T(1,128)S(1)}, u32[]{:S(2)}, u32[]{:S(2)}) collective-permute-start(f32[1,2048]{1,0:T(1,128)S(1)} %get-tuple-element.91), channel_id=1, source_target_pairs={{0,8},{1,9},{2,10},{3,11},{4,12},{5,13},{6,14},{7,15},{16,24},{17,... | collective-permute-start | bytes 24584 | tf_op jit(solution)/shard_map/ppermute | solution.py:45
  153.9 6.4 %collective-permute-start.17 = (f32[1,2048]{1,0:T(1,128)S(1)}, f32[1,2048]{1,0:T(1,128)S(1)}, u32[]{:S(2)}, u32[]{:S(2)}) collective-permute-start(f32[1,2048]{1,0:T(1,128)S(1)} %get-tuple-element.92), channel_id=1, source_target_pairs={{8,0},{9,1},{10,2},{11,3},{12,4},{13,5},{14,6},{15,7},{24,16},{25,... | collective-permute-start | bytes 24584 | tf_op jit(solution)/shard_map/ppermute | solution.py:45
  160.5 4.0 %collective-permute-start.19 = (f32[4,1,2048]{2,0,1:T(4,128)S(1)}, f32[4,1,2048]{2,0,1:T(4,128)S(1)}, u32[]{:S(2)}, u32[]{:S(2)}) collective-permute-start(f32[4,1,2048]{2,0,1:T(4,128)S(1)} %select_bitcast_fusion), channel_id=1, source_target_pairs={{0,4},{1,5},{2,6},{3,7},{4,0},{5,1},{6,2},{7,3},{8,12},{9,13},{10,... | collective-permute-start | bytes 98312 | tf_op jit(solution)/shard_map/ppermute | solution.py:35
  164.5 3.8 %collective-permute-start.20 = (f32[2,1,2048]{2,0,1:T(2,128)S(1)}, f32[2,1,2048]{2,0,1:T(2,128)S(1)}, u32[]{:S(2)}, u32[]{:S(2)}) collective-permute-start(f32[2,1,2048]{2,0,1:T(2,128)S(1)} %broadcast_select_fusion.4), channel_id=1, source_target_pairs={{0,2},{1,3},{2,0},{3,1},{4,6},{5,7},{6,4},{7,5},{8,10},{9,11},{10,... | collective-permute-start | bytes 49160 | tf_op jit(solution)/shard_map/ppermute | solution.py:35
  168.3 59.8 %collective-permute-start.21 = (f32[1,1,2048]{2,0,1:T(1,128)S(1)}, f32[1,1,2048]{2,0,1:T(1,128)S(1)}, u32[]{:S(2)}, u32[]{:S(2)}) collective-permute-start(f32[1,1,2048]{2,0,1:T(1,128)S(1)} %broadcast_select_fusion.5), channel_id=1, source_target_pairs={{0,1},{1,0},{2,3},{3,2},{4,5},{5,4},{6,7},{7,6},{8,9},{9,8},{10,11... | collective-permute-start | bytes 24584 | tf_op jit(solution)/shard_map/ppermute | solution.py:35
where the time goes:
time: 230 us; the launch traced here: 229 us
  blocking collectives  59.7 us (26%)
  starting transfers between devices  56.9 us (25%)
  local copies, waits for them, and re-layouts  31.1 us (14%)
  other arithmetic  28.9 us (13%)
  waiting for transfers between devices  20.4 us (9%)
  between operations  16.9 us (7%)
  matrix products  14.7 us (6%)
    psum x1, blocking collectives, body(): traces = lax.psum(own_traces, 'slab')  59.7 us
    ppermute x10, starting transfers between devices, from_behind(): lax.ppermute(value, axis, [(source, source + steps) for source in range(l...  26.7 us
    ppermute x3, starting transfers between devices, extended_2(): lax.ppermute(lax.slice_in_dim(block, block.shape[dim] - width, None, axis...  15.9 us
    dot_general x54, matrix products, conv_taps(): jnp.einsum('oi,izn->ozn', weight[tap_index], piece * column_valid, prefer...  14.4 us
    ppermute x10, waiting for transfers between devices, from_behind(): lax.ppermute(value, axis, [(source, source + steps) for source in range(l...  14.1 us
    add x4, other arithmetic, body(): advanced = 2.0 * current - previous + courant_sq * laplace_term  12.9 us
    ppermute x6, starting transfers between devices, from_partner(): return lax.ppermute(value, axis, pairs)  10.4 us
    gather x4, local copies, waits for them, and re-layouts, body(): advanced[station_depth, station[1], station[2]]  5.93 us
  transfers between devices with their start and end apart: 22, of which 9 were waited for; matrix products, arithmetic and copies ran while one was open for 10% of the time, Pallas kernels for 0%

commit v1 on v0

v1 whole, which is shorter than its diff:
```python
import functools

import jax
import jax.numpy as jnp
import numpy as np
from jax import lax
from jax.experimental import pallas as pl
from jax.experimental.pallas import tpu as pltpu
from jax.sharding import PartitionSpec as P

CY = 32
CX = 64
CELLS = CY * CX
CH = 64
SHOTS = 8
STEPS = 4
FPS = 16
FY = 64
FX = 128
PARTS = 4

C = (-205.0 / 72.0, 8.0 / 5.0, -1.0 / 5.0, 8.0 / 315.0, -1.0 / 560.0)
COURANT = 0.088
LEAK = 0.2
F32 = jnp.float32
BF16 = jnp.bfloat16


def banded(n):
    t = np.zeros((n, n), np.float64)
    for k in range(5):
        for i in range(n):
            for j in {i - k, i + k}:
                if 0 <= j < n:
                    t[i, j] = C[k]
    hi = t.astype(jnp.bfloat16).astype(np.float64)
    return hi, t - hi


def doubling(n):
    u = np.zeros((2 * n, n))
    for k in range(n):
        u[2 * k, k] += 0.75
        u[2 * k, max(k - 1, 0)] += 0.25
        u[2 * k + 1, k] += 0.75
        u[2 * k + 1, min(k + 1, n - 1)] += 0.25
    return u


def constants():
    hi, lo = banded(FX)
    along_x = np.concatenate([hi, hi, lo], axis=0)
    hi, lo = banded(FY)
    four = np.eye(4)
    along_y = np.concatenate([np.kron(four, hi), np.kron(four, hi), np.kron(four, lo)], axis=1)
    depth = np.zeros((FPS, SHOTS + 2))
    for k in range(SHOTS):
        depth[2 * k, k + 1] = 0.75
        depth[2 * k, k] = 0.25
        depth[2 * k + 1, k + 1] = 0.75
        depth[2 * k + 1, k + 2] = 0.25
    rows = doubling(CY)
    up_zy = np.concatenate([np.kron(depth, rows[:, 0::2]), np.kron(depth, rows[:, 1::2])], axis=1)
    up_x = np.kron(np.eye(2), doubling(CX).T)
    out = (along_x, along_y, up_zy, up_zy.T, up_x, up_x.T)
    return [jnp.asarray(a.astype(jnp.bfloat16)) for a in out]


def dot(a, b, dims=((1,), (0,))):
    return lax.dot_general(a, b, (dims, ((), ())), preferred_element_type=F32)


def two(v):
    hi = v.astype(BF16)
    return hi, (v - hi.astype(F32)).astype(BF16)


def kernel(
    n,
    latent,
    w1,
    w2,
    head,
    wavelet,
    sources,
    receivers,
    along_x,
    along_y,
    up_x,
    up_xt,
    prev_hbm,
    cur_hbm,
    adj_hbm,
    up_zy_hbm,
    up_zyt_hbm,
    final_out,
    traces_out,
    gradient_out,
    a1,
    a2,
    wp1,
    wp2,
    y,
    vel,
    vels,
    field,
    adj,
    up_zy,
    up_zyt,
    speed,
    corr,
    rim_out,
    rim_in,
    hot,
    rec,
    recs,
    gr,
    grs,
    total,
    local_sem,
    lat_s,
    lat_r,
    hid_s,
    hid_r,
    rim_s,
    rim_r,
    vel_s,
    vel_r,
    rec_s,
    rec_r,
    gr_s,
    gr_r,
):
    me = lax.axis_index("slab")
    shot = lax.rem(me, SHOTS)
    slab = me // SHOTS
    slabs = n // SHOTS
    has_low = slab > 0
    has_high = slab < slabs - 1
    steps_here = range(STEPS)

    inner = pl.ds(4, FPS)
    loads = [
        pltpu.make_async_copy(cur_hbm, field.at[1, inner], local_sem.at[0]),
        pltpu.make_async_copy(prev_hbm, field.at[0, inner], local_sem.at[1]),
        pltpu.make_async_copy(up_zy_hbm, up_zy, local_sem.at[2]),
        pltpu.make_async_copy(adj_hbm, adj, local_sem.at[3]),
        pltpu.make_async_copy(up_zyt_hbm, up_zyt, local_sem.at[4]),
    ]
    for load in loads:
        load.start()

    def remote(src, dst, send, recv, target):
        return pltpu.make_async_remote_copy(
            src_ref=src,
            dst_ref=dst,
            send_sem=send,
            recv_sem=recv,
            device_id={"slab": target},
            device_id_type=pl.DeviceIdType.MESH,
        )

    def peer(j):
        return lax.rem(me + j, n)

    barrier = pltpu.get_barrier_semaphore()

    def greet(j, carry):
        pl.semaphore_signal(
            barrier, inc=1, device_id={"slab": peer(j)}, device_id_type=pl.DeviceIdType.MESH
        )
        return carry

    lax.fori_loop(1, n, greet, 0)

    for a in (a1, a2):

        @pl.when(me == 0)
        def _():
            a[0] = jnp.zeros((CH, CELLS), BF16)

        @pl.when(me == n - 1)
        def _():
            a[2] = jnp.zeros((CH, CELLS), BF16)

    a1[1] = latent[...]
    pl.semaphore_wait(barrier, n - 1)

    width = CELLS // PARTS

    def lat_copy(side, part):
        cols = pl.ds(part * width, width)
        return remote(
            latent.at[:, cols],
            a1.at[2 * side, :, cols],
            lat_s.at[side, part],
            lat_r.at[side, part],
            peer(1 if side == 0 else n - 1),
        )

    height = CH // PARTS

    def hid_copy(side, part):
        rows = pl.ds(pl.multiple_of(part * height, height), height)
        return remote(
            a2.at[1, rows],
            a2.at[2 * side, rows],
            hid_s.at[side, part],
            hid_r.at[side, part],
            peer(1 if side == 0 else n - 1),
        )

    def rim_copy(side, step):
        return remote(
            rim_out.at[side, step],
            rim_in.at[side, step],
            rim_s.at[side, step],
            rim_r.at[side, step],
            peer(SHOTS if side == 0 else n - SHOTS),
        )

    sends = (me < n - 1, me > 0)
    gets = (me > 0, me < n - 1)
    rim_sends = (has_high, has_low)
    rim_gets = (has_low, has_high)

    for part in range(PARTS):
        for side in range(2):

            @pl.when(sends[side])
            def _():
                lat_copy(side, part).start()

    for w, packed in ((w1, wp1), (w2, wp2)):
        for tap in range(9):
            for dz in range(3):
                packed[tap * CH : (tap + 1) * CH, dz * CH : (dz + 1) * CH] = w[dz * 9 + tap]

    loads[0].wait()
    rim_out[0, 0] = field[1, FPS : FPS + 4].reshape(4 * FY, FX).astype(BF16)
    rim_out[1, 0] = field[1, 4:8].reshape(4 * FY, FX).astype(BF16)
    for side in range(2):

        @pl.when(rim_sends[side])
        def _():
            rim_copy(side, 0).start()

    @pl.when(jnp.logical_not(has_low))
    def _():
        field[:, 0:4] = jnp.zeros((2, 4, FY, FX), F32)

    @pl.when(jnp.logical_not(has_high))
    def _():
        field[:, FPS + 4 :] = jnp.zeros((2, 4, FY, FX), F32)

    corr[...] = jnp.zeros((FPS * FY, FX), F32)
    station = receivers[shot]
    station_row = (station[0:1] - slab * FPS) * FY + station[1:2]
    station_col = station[2:3]
    hot[...] = (
        (lax.broadcasted_iota(jnp.int32, (FPS * FY, FX), 0) == station_row)
        .astype(F32)
        .astype(BF16)
    )
    col_hot = (lax.broadcasted_iota(jnp.int32, (FX, FX), 0) == station_col).astype(F32)
    rec[...] = jnp.zeros((8, FX), F32)

    cell = lax.broadcasted_iota(jnp.int32, (1, CELLS), 1)
    col = lax.rem(cell, CX)
    keep_left = (col > 0).astype(F32)
    keep_right = (col < CX - 1).astype(F32)
    keep_up = (cell >= CX).astype(F32)
    keep_down = (cell < CELLS - CX).astype(F32)

    def multiply(packed, a, part):
        cols = slice(part * width, (part + 1) * width)
        block = jnp.concatenate([a[0, :, cols], a[1, :, cols], a[2, :, cols]], axis=0)
        y[:, :, cols] = dot(packed[...], block).reshape(9, CH, width)

    def gathered(first):
        sums = []
        for dx in range(3):
            above = y[dx, pl.ds(first, 8)]
            middle = y[3 + dx, pl.ds(first, 8)]
            below = y[6 + dx, pl.ds(first, 8)]
            sums.append(
                middle
                + keep_up * pltpu.roll(above, CX, 1)
                + keep_down * pltpu.roll(below, CELLS - CX, 1)
            )
        v = (
            sums[1]
            + keep_left * pltpu.roll(sums[0], 1, 1)
            + keep_right * pltpu.roll(sums[2], CELLS - 1, 1)
        )
        return jnp.where(v > 0, v, LEAK * v)

    for part in range(PARTS):
        for side in range(2):

            @pl.when(gets[side])
            def _():
                lat_copy(side, part).wait_recv()

        multiply(wp1, a1, part)

    def hidden_part(part, carry):
        first = pl.multiple_of(part * height, height)
        pieces = [gathered(pl.multiple_of(first + 8 * h, 8)) for h in range(height // 8)]
        a2[1, pl.ds(first, height)] = jnp.concatenate(pieces, axis=0).astype(BF16)
        for side in range(2):

            @pl.when(sends[side])
            def _():
                hid_copy(side, part).start()

        return carry

    lax.fori_loop(0, PARTS, hidden_part, 0)
    for part in range(PARTS):
        for side in range(2):

            @pl.when(gets[side])
            def _():
                hid_copy(side, part).wait_recv()

    for part in range(PARTS):
        multiply(wp2, a2, part)

    def logit_part(part, acc):
        first = pl.multiple_of(part * 8, 8)
        return acc + head[pl.ds(first, 8), 0:1] * gathered(first)

    logits = jnp.sum(
        lax.fori_loop(0, CH // 8, logit_part, jnp.zeros((8, CELLS), F32)), axis=0, keepdims=True
    )
    wave_speed = 1.5 + 3.0 / (1.0 + jnp.exp(-logits))
    rows16 = jnp.concatenate(
        [wave_speed[:, FX * j : FX * (j + 1)] for j in range(CELLS // FX)], axis=0
    )
    vel[...] = rows16.astype(BF16)

    def vel_copy(j):
        return remote(vel, vels.at[j], vel_s.at[j], vel_r.at[j], peer(j))

    def rec_copy(j):
        return remote(rec, recs.at[j], rec_s.at[j], rec_r.at[j], peer(j))

    def over_peers(what):
        def one(j, carry):
            what(j)
            return carry

        lax.fori_loop(1, n, one, 0)

    over_peers(lambda j: vel_copy(j).start())
    vels[0] = vel[...]
    over_peers(lambda j: vel_copy(j).wait_recv())

    planes = []
    for i in range(SHOTS + 2):
        plane = jnp.clip(slab * SHOTS - 1 + i, 0, n - 1)
        planes.append(vels[lax.rem(me - plane + n, n)])
    wide = dot(jnp.concatenate(planes, axis=0), up_x[...])
    tall = jnp.concatenate([wide[:, :FX], wide[:, FX:]], axis=0)
    hi, lo = two(tall)
    loads[2].wait()
    speed[...] = dot(up_zy[...], hi) + dot(up_zy[...], lo)

    loads[1].wait()
    loads[3].wait()
    source_at = (
        (sources[shot, 0] - slab * FPS) * (FY * FX) + sources[shot, 1] * FX + sources[shot, 2]
    )
    linear = lax.broadcasted_iota(jnp.int32, (4 * FY, FX), 0) * FX + lax.broadcasted_iota(
        jnp.int32, (4 * FY, FX), 1
    )

    def pair(t, cur, old, chunks):
        centres = [field[cur, 4 + 4 * c : 8 + 4 * c].reshape(4 * FY, FX) for c in chunks]
        halves = [two(v) for v in centres]
        across = jnp.concatenate(
            [jnp.concatenate([hi, lo, hi], axis=0) for hi, lo in halves], axis=1
        )
        from_rows = dot(along_y[...], across)
        for i, c in enumerate(chunks):
            v = centres[i]
            hi, lo = halves[i]
            lap = from_rows[:, FX * i : FX * (i + 1)]
            lap = lap + dot(jnp.concatenate([hi, lo, hi], axis=1), along_x[...])
            lap = lap + C[0] * v
            at = 4 + 4 * c
            for k in range(1, 5):
                near = field[cur, at - k : at - k + 4] + field[cur, at + k : at + k + 4]
                lap = lap + C[k] * near.reshape(4 * FY, FX)
            rows = slice(4 * FY * c, 4 * FY * (c + 1))
            courant = COURANT * speed[rows]
            pulse = jnp.where(linear == source_at - c * 4 * FY * FX, wavelet[shot, t], 0.0)
            before = field[old, at : at + 4].reshape(4 * FY, FX)
            new = 2.0 * v - before + courant * courant * lap + pulse
            corr[rows] += adj[t, 4 * c : 4 * c + 4].reshape(4 * FY, FX).astype(F32) * lap
            field[old, at : at + 4] = new.reshape(4, FY, FX)

    def step(t, carry):
        cur = lax.rem(t + 1, 2)
        old = lax.rem(t, 2)
        for side in range(2):

            @pl.when(rim_gets[side])
            def _():
                rim_copy(side, t).wait_recv()
                at = (FPS + 4) * side
                field[cur, at : at + 4] = rim_in[side, t].reshape(4, FY, FX).astype(F32)

        pair(t, cur, old, (0, 3))

        @pl.when(t < STEPS - 1)
        def _():
            rim_out[0, t + 1] = field[old, FPS : FPS + 4].reshape(4 * FY, FX).astype(BF16)
            rim_out[1, t + 1] = field[old, 4:8].reshape(4 * FY, FX).astype(BF16)
            for side in range(2):

                @pl.when(rim_sends[side])
                def _():
                    rim_copy(side, t + 1).start()

        pair(t, cur, old, (1, 2))
        hi, lo = two(field[old, 4 : 4 + FPS].reshape(FPS * FY, FX))
        seen = dot(hi, hot[...], ((0,), (0,))) + dot(lo, hot[...], ((0,), (0,)))
        seen = jnp.sum(seen * col_hot, axis=0, keepdims=True)
        rec[...] += jnp.where(lax.broadcasted_iota(jnp.int32, (8, FX), 0) == t, seen, 0.0)
        return carry

    lax.fori_loop(0, STEPS, step, 0)
    over_peers(lambda j: rec_copy(j).start())

    fine = (2.0 * COURANT * COURANT) * speed[...] * corr[...]
    hi, lo = two(fine)
    loads[4].wait()
    tall = dot(up_zyt[...], hi) + dot(up_zyt[...], lo)
    half = tall.shape[0] // 2
    hi, lo = two(jnp.concatenate([tall[:half], tall[half:]], axis=1))
    narrow = dot(hi, up_xt[...]) + dot(lo, up_xt[...])
    gr[...] = narrow.reshape(SHOTS + 2, 16, FX)

    @pl.when(jnp.logical_not(has_low))
    def _():
        gr[1] += gr[0]

    @pl.when(jnp.logical_not(has_high))
    def _():
        gr[SHOTS] += gr[SHOTS + 1]

    def gr_copy(j):
        other = lax.rem(shot + j, SHOTS)
        return remote(
            gr.at[other + 1], grs.at[j], gr_s.at[j], gr_r.at[j], slab * SHOTS + other
        )

    def low_copy(slot):
        return remote(
            gr.at[0], grs.at[slot], gr_s.at[8], gr_r.at[slot], lax.rem(slab * SHOTS - 1 + n, n)
        )

    def high_copy(slot):
        return remote(
            gr.at[SHOTS + 1],
            grs.at[slot],
            gr_s.at[9],
            gr_r.at[slot],
            lax.rem((slab + 1) * SHOTS, n),
        )

    @pl.when(has_low)
    def _():
        low_copy(8 + shot).start()

    @pl.when(has_high)
    def _():
        high_copy(16 + shot).start()

    for j in range(1, SHOTS):
        gr_copy(j).start()

    final_out[...] = field[(STEPS + 1) % 2, 4 : 4 + FPS]

    recs[0] = rec[...]
    over_peers(lambda j: rec_copy(j).wait_recv())
    for s in range(SHOTS):

        def slab_term(k, acc):
            return acc + recs[lax.rem(me - (k * SHOTS + s) + n, n)]

        summed = lax.fori_loop(0, slabs, slab_term, jnp.zeros((8, FX), F32))
        traces_out[s] = summed[:STEPS]

    total[...] = gr[shot + 1]
    for j in range(1, SHOTS):
        gr_copy(j).wait_recv()
        total[...] += grs[j]

    @pl.when((shot == SHOTS - 1) & has_high)
    def _():
        for s in range(SHOTS):
            low_copy(8 + s).wait_recv()
            total[...] += grs[8 + s]

    @pl.when((shot == 0) & has_low)
    def _():
        for s in range(SHOTS):
            high_copy(16 + s).wait_recv()
            total[...] += grs[16 + s]

    gradient_out[...] = total[...]

    for part in range(PARTS):
        for side in range(2):

            @pl.when(sends[side])
            def _():
                lat_copy(side, part).wait_send()
                hid_copy(side, part).wait_send()

    for t in steps_here:
        for side in range(2):

            @pl.when(rim_sends[side])
            def _():
                rim_copy(side, t).wait_send()

    over_peers(lambda j: vel_copy(j).wait_send())
    over_peers(lambda j: rec_copy(j).wait_send())
    for j in range(1, SHOTS):
        gr_copy(j).wait_send()

    @pl.when(has_low)
    def _():
        low_copy(8 + shot).wait_send()

    @pl.when(has_high)
    def _():
        high_copy(16 + shot).wait_send()


def body(
    n,
    latent,
    conv1_weight,
    conv2_weight,
    head,
    p_prev,
    p_cur,
    adjoint,
    wavelet,
    sources,
    receivers,
):
    along_x, along_y, up_zy, up_zyt, up_x, up_xt = constants()
    vmem = pl.BlockSpec(memory_space=pltpu.VMEM)
    smem = pl.BlockSpec(memory_space=pltpu.SMEM)
    hbm = pl.BlockSpec(memory_space=pl.ANY)
    dma = pltpu.SemaphoreType.DMA
    final, traces, gradient = pl.pallas_call(
        functools.partial(kernel, n),
        out_shape=(
            jax.ShapeDtypeStruct((FPS, FY, FX), F32),
            jax.ShapeDtypeStruct((SHOTS, STEPS, 128), F32),
            jax.ShapeDtypeStruct((16, FX), F32),
        ),
        in_specs=[vmem] * 4 + [smem] * 2 + [vmem] * 5 + [hbm] * 5,
        out_specs=(vmem, vmem, vmem),
        scratch_shapes=[
            pltpu.VMEM((3, CH, CELLS), BF16),
            pltpu.VMEM((3, CH, CELLS), BF16),
            pltpu.VMEM((9 * CH, 3 * CH), BF16),
            pltpu.VMEM((9 * CH, 3 * CH), BF16),
            pltpu.VMEM((9, CH, CELLS), F32),
            pltpu.VMEM((16, FX), BF16),
            pltpu.VMEM((n, 16, FX), BF16),
            pltpu.VMEM((2, FPS + 8, FY, FX), F32),
            pltpu.VMEM((STEPS, FPS, FY, FX), BF16),
            pltpu.VMEM(up_zy.shape, BF16),
            pltpu.VMEM(up_zyt.shape, BF16),
            pltpu.VMEM((FPS * FY, FX), F32),
            pltpu.VMEM((FPS * FY, FX), F32),
            pltpu.VMEM((2, STEPS, 4 * FY, FX), BF16),
            pltpu.VMEM((2, STEPS, 4 * FY, FX), BF16),
            pltpu.VMEM((FPS * FY, FX), BF16),
            pltpu.VMEM((8, FX), F32),
            pltpu.VMEM((n, 8, FX), F32),
            pltpu.VMEM((SHOTS + 2, 16, FX), F32),
            pltpu.VMEM((3 * SHOTS, 16, FX), F32),
            pltpu.VMEM((16, FX), F32),
            dma((5,)),
            dma((2, PARTS)),
            dma((2, PARTS)),
            dma((2, PARTS)),
            dma((2, PARTS)),
            dma((2, STEPS)),
            dma((2, STEPS)),
            dma((n,)),
            dma((n,)),
            dma((n,)),
            dma((n,)),
            dma((10,)),
            dma((3 * SHOTS,)),
        ],
        compiler_params=pltpu.CompilerParams(
            collective_id=0, has_side_effects=True, vmem_limit_bytes=48 * 2**20
        ),
    )(
        latent.reshape(CH, CELLS),
        conv1_weight,
        conv2_weight,
        jnp.broadcast_to(head.astype(F32)[:, None], (CH, 128)),
        wavelet,
        sources,
        receivers,
        along_x,
        along_y,
        up_x,
        up_xt,
        p_prev[0],
        p_cur[0],
        adjoint[:, 0],
        up_zy,
        up_zyt,
    )
    return final[None], traces, gradient.reshape(1, CELLS)


def solution(mesh):
    in_specs = (
        P(None, ("groups", "slab"), None),
        P(),
        P(),
        P(),
        P(("groups", "slab"), None, None, None),
        P(("groups", "slab"), None, None, None),
        P(None, ("groups", "slab"), None, None, None),
        P("groups", None),
        P("groups", None),
        P("groups", None, None),
    )
    out_specs = (
        P(("groups", "slab"), None, None, None),
        P("groups", None, None),
        P(("groups", "slab"), None),
    )
    return jax.shard_map(
        functools.partial(body, mesh.shape["slab"]),
        mesh=mesh,
        in_specs=in_specs,
        out_specs=out_specs,
        check_vma=False,
    )
```

time: 230 us -> 69.3 us (0.30)
  blocking collectives: 59.7 us -> 0 us
  starting transfers between devices: 56.9 us -> 0 us
  Pallas kernels: 0 us -> 51.7 us
  other arithmetic: 28.9 us -> 0 us
  waiting for transfers between devices: 20.4 us -> 0 us
  between operations: 16.9 us -> 0.66 us
  local copies, waits for them, and re-layouts: 31.1 us -> 16.2 us
  matrix products: 14.7 us -> 0 us
    psum x1 -> x0, blocking collectives: 59.7 us -> none  [body(): traces = lax.psum(own_traces, 'slab')]
    ppermute x22 -> x0, starting transfers between devices: 56.9 us -> none  [the longest x10 26.7 us: from_behind(): lax.ppermute(value, axis, [(source, source + steps) for source in range(l...]
    pallas_call x0 -> x1, Pallas kernels: none -> 51.7 us  [body(): pl.pallas_call(functools.partial(kernel, n), out_shape=(jax.ShapeDtypeStr...]
    ppermute x22 -> x0, waiting for transfers between devices: 20.4 us -> none  [the longest x10 14.1 us: from_behind(): lax.ppermute(value, axis, [(source, source + steps) for source in range(l...]
    add x9 -> x0, other arithmetic: 14.8 us -> none  [the longest x4 12.9 us: body(): advanced = 2.0 * current - previous + courant_sq * laplace_term]
    dot_general x55 -> x0, matrix products: 14.7 us -> none  [the longest x54 14.4 us: conv_taps(): jnp.einsum('oi,izn->ozn', weight[tap_index], piece * column_valid, prefer...]
    unnamed x63 -> x30, local copies, waits for them, and re-layouts: 3.56 us -> 15.5 us
    mul x4 -> x0, local copies, waits for them, and re-layouts: 6.2 us -> none  [the longest x3 5.89 us: body(): fine_gradient = 2.0 * courant * courant * fine_speed * correlation]
  transfers between devices with their start and end apart: 22 -> 0, of which waited for: 9 -> 0; matrix products, arithmetic and copies ran while one was open for 10% -> 0% of each run, Pallas kernels for 0% -> 0%
where the time goes in v1:
time: 69.3 us; the launch traced here: 68.6 us
  Pallas kernels  51.7 us (75%)
  local copies, waits for them, and re-layouts  16.2 us (23%)
    pallas_call x1, Pallas kernels, body(): pl.pallas_call(functools.partial(kernel, n), out_shape=(jax.ShapeDtypeStr...  51.7 us
    unnamed x30, local copies, waits for them, and re-layouts  15.5 us

profile of v1, /device:TPU:0, one launch (start us, length us, event | category | flops | bytes accessed | tf_op | source)
XLA Modules:
  0.0 68.6 jit_solution(14586889107019675442)
XLA Ops:
  0.6 0.0 copy-start.10
  0.6 0.8 %copy.19.wavelet = f32[8,4]{1,0:T(8,128)S(1)} copy(f32[8,4]{0,1:T(4,128)} %param.23) | data formatting | bytes 256 | tf_op args[7]
  1.4 0.8 %copy.20.sources = s32[8,3]{1,0:T(8,128)S(1)} copy(s32[8,3]{0,1:T(4,128)} %param.24) | data formatting | bytes 192 | tf_op args[8]
  2.2 0.7 %copy.21.receivers = s32[8,3,128]{2,1,0:T(4,128)S(1)} copy(s32[8,3,128]{2,0,1:T(8,128)} %param.25) | data formatting | bytes 24576 | tf_op args[9]
  2.9 0.7 %broadcast_in_dim.4.head = f32[64,128]{1,0:T(8,128)S(1)} broadcast(bf16[64]{0:T(256)(128)(2,1)} %param.19), dimensions={0} | broadcast | bytes 32896 | tf_op jit(solution)/shard_map/broadcast_in_dim | solution.py:615
  3.6 0.0 copy-done.10
  3.6 0.0 copy-start
  3.6 1.2 %copy-done = bf16[4,1,16,64,128]{4,3,2,1,0:T(8,128)(2,1)S(1)} copy-done((bf16[4,1,16,64,128]{4,3,2,1,0:T(8,128)(2,1)S(1)}, bf16[4,1,16,64,128]{4,3,2,1,0:T(8,128)(2,1)}, u32[]{:S(2)}) %copy-start) | copy-done | bytes 1048600
  4.9 0.0 copy-start.1
  4.9 1.1 %copy-done.1 = bf16[1024,320]{1,0:T(8,128)(2,1)S(1)} copy-done((bf16[1024,320]{1,0:T(8,128)(2,1)S(1)}, bf16[1024,320]{1,0:T(8,128)(2,1)}, u32[]{:S(2)}) %copy-start.1) | copy-done | bytes 655384
  6.0 0.0 copy-start.2
  6.0 1.1 %copy-done.2 = bf16[320,1024]{1,0:T(8,128)(2,1)S(1)} copy-done((bf16[320,1024]{1,0:T(8,128)(2,1)S(1)}, bf16[320,1024]{1,0:T(8,128)(2,1)}, u32[]{:S(2)}) %copy-start.2) | copy-done | bytes 655384
  7.1 0.0 copy-start.3
  7.1 1.0 %copy-done.3 = f32[1,16,64,128]{3,2,1,0:T(8,128)S(1)} copy-done((f32[1,16,64,128]{3,2,1,0:T(8,128)S(1)}, f32[1,16,64,128]{3,2,1,0:T(8,128)}, u32[]{:S(2)}) %copy-start.3) | copy-done | bytes 524312
  8.1 0.0 copy-start.4
  8.1 1.0 %copy-done.4 = f32[1,16,64,128]{3,2,1,0:T(8,128)S(1)} copy-done((f32[1,16,64,128]{3,2,1,0:T(8,128)S(1)}, f32[1,16,64,128]{3,2,1,0:T(8,128)}, u32[]{:S(2)}) %copy-start.4) | copy-done | bytes 524312
  9.2 0.0 copy-start.5
  9.2 1.0 %copy-done.5 = bf16[27,64,64]{2,1,0:T(8,128)(2,1)S(1)} copy-done((bf16[27,64,64]{2,1,0:T(8,128)(2,1)S(1)}, bf16[27,64,64]{2,1,0:T(8,128)(2,1)}, u32[]{:S(2)}) %copy-start.5) | copy-done | bytes 221208
  10.2 0.0 copy-start.6
  10.2 1.0 %copy-done.6 = bf16[27,64,64]{2,1,0:T(8,128)(2,1)S(1)} copy-done((bf16[27,64,64]{2,1,0:T(8,128)(2,1)S(1)}, bf16[27,64,64]{2,1,0:T(8,128)(2,1)}, u32[]{:S(2)}) %copy-start.6) | copy-done | bytes 221208
  11.2 0.0 copy-start.7
  11.2 1.0 %copy-done.7 = bf16[256,768]{1,0:T(8,128)(2,1)S(1)} copy-done((bf16[256,768]{1,0:T(8,128)(2,1)S(1)}, bf16[256,768]{1,0:T(8,128)(2,1)}, u32[]{:S(2)}) %copy-start.7) | copy-done | bytes 393240
  12.2 0.0 copy-start.8
  12.2 0.9 %copy-done.8 = bf16[64,1,2048]{2,0,1:T(8,128)(2,1)S(1)} copy-done((bf16[64,1,2048]{2,0,1:T(8,128)(2,1)S(1)}, bf16[64,1,2048]{2,0,1:T(8,128)(2,1)}, u32[]{:S(2)}) %copy-start.8) | copy-done | bytes 262168
  13.1 0.0 copy-start.9
  13.1 0.9 %copy-done.9 = bf16[384,128]{1,0:T(8,128)(2,1)S(1)} copy-done((bf16[384,128]{1,0:T(8,128)(2,1)S(1)}, bf16[384,128]{1,0:T(8,128)(2,1)}, u32[]{:S(2)}) %copy-start.9) | copy-done | bytes 98328
  14.0 0.0 copy-start.11
  14.0 0.8 %copy-done.11 = bf16[128,256]{1,0:T(8,128)(2,1)S(1)} copy-done((bf16[128,256]{1,0:T(8,128)(2,1)S(1)}, bf16[128,256]{1,0:T(8,128)(2,1)}, u32[]{:S(2)}) %copy-start.11) | copy-done | bytes 65560
  14.9 51.7 %shard_map.175 = (f32[16,64,128]{2,1,0:T(8,128)S(1)}, f32[8,4,128]{2,1,0:T(4,128)S(1)}, f32[16,128]{1,0:T(8,128)S(1)}) custom-call(bf16[64,2048]{1,0:T(8,128)(2,1)S(1)} %bitcast.10, bf16[27,64,64]{2,1,0:T(8,128)(2,1)S(1)} %copy-done.5, bf16[27,64,64]{2,1,0:T(8,128)(2,1)S(1)} %copy-done.6, f32[64,128]{1,0:T(8,128)S(1)} %broadcast_in_dim.4.head, ...), custom_call_target="tpu_custom_call" | custom-call | tf_op jit(solution)/shard_map/pallas_call | solution.py:563
  66.6 0.8 %copy.25 = f32[1,16,64,128]{3,2,1,0:T(8,128)} copy(f32[1,16,64,128]{3,2,1,0:T(8,128)S(1)} %bitcast.7) | data formatting | bytes 1048576
  67.4 0.6 copy.26
  68.0 0.6 copy.27
Async XLA Ops:
  0.6 3.0 %copy-start.10 = (bf16[256,128]{1,0:T(8,128)(2,1)S(1)}, bf16[256,128]{1,0:T(8,128)(2,1)}, u32[]{:S(2)}) copy-start(bf16[256,128]{1,0:T(8,128)(2,1)} %constant.17.clone.up_xt) | copy-start | bytes 196612
  3.6 1.2 %copy-start = (bf16[4,1,16,64,128]{4,3,2,1,0:T(8,128)(2,1)S(1)}, bf16[4,1,16,64,128]{4,3,2,1,0:T(8,128)(2,1)}, u32[]{:S(2)}) copy-start(bf16[4,1,16,64,128]{4,3,2,1,0:T(8,128)(2,1)} %param.22) | copy-start | bytes 3145732
  4.9 1.1 %copy-start.1 = (bf16[1024,320]{1,0:T(8,128)(2,1)S(1)}, bf16[1024,320]{1,0:T(8,128)(2,1)}, u32[]{:S(2)}) copy-start(bf16[1024,320]{1,0:T(8,128)(2,1)} %constant.14.clone.up_zy_hbm) | copy-start | bytes 1966084
  6.0 1.1 %copy-start.2 = (bf16[320,1024]{1,0:T(8,128)(2,1)S(1)}, bf16[320,1024]{1,0:T(8,128)(2,1)}, u32[]{:S(2)}) copy-start(bf16[320,1024]{1,0:T(8,128)(2,1)} %constant.15.clone.up_zyt_hbm) | copy-start | bytes 1966084
  7.1 1.0 %copy-start.3 = (f32[1,16,64,128]{3,2,1,0:T(8,128)S(1)}, f32[1,16,64,128]{3,2,1,0:T(8,128)}, u32[]{:S(2)}) copy-start(f32[1,16,64,128]{3,2,1,0:T(8,128)} %param.20) | copy-start | bytes 1572868
  8.1 1.0 %copy-start.4 = (f32[1,16,64,128]{3,2,1,0:T(8,128)S(1)}, f32[1,16,64,128]{3,2,1,0:T(8,128)}, u32[]{:S(2)}) copy-start(f32[1,16,64,128]{3,2,1,0:T(8,128)} %param.21) | copy-start | bytes 1572868
  9.2 1.0 %copy-start.5 = (bf16[27,64,64]{2,1,0:T(8,128)(2,1)S(1)}, bf16[27,64,64]{2,1,0:T(8,128)(2,1)}, u32[]{:S(2)}) copy-start(bf16[27,64,64]{2,1,0:T(8,128)(2,1)} %w1.1) | copy-start | bytes 663556
  10.2 1.0 %copy-start.6 = (bf16[27,64,64]{2,1,0:T(8,128)(2,1)S(1)}, bf16[27,64,64]{2,1,0:T(8,128)(2,1)}, u32[]{:S(2)}) copy-start(bf16[27,64,64]{2,1,0:T(8,128)(2,1)} %w2.1) | copy-start | bytes 663556
  11.2 1.0 %copy-start.7 = (bf16[256,768]{1,0:T(8,128)(2,1)S(1)}, bf16[256,768]{1,0:T(8,128)(2,1)}, u32[]{:S(2)}) copy-start(bf16[256,768]{1,0:T(8,128)(2,1)} %constant.13.clone.along_y) | copy-start | bytes 1179652
  12.2 0.9 %copy-start.8 = (bf16[64,1,2048]{2,0,1:T(8,128)(2,1)S(1)}, bf16[64,1,2048]{2,0,1:T(8,128)(2,1)}, u32[]{:S(2)}) copy-start(bf16[64,1,2048]{2,0,1:T(8,128)(2,1)} %param.16) | copy-start | bytes 786436
  13.1 0.9 %copy-start.9 = (bf16[384,128]{1,0:T(8,128)(2,1)S(1)}, bf16[384,128]{1,0:T(8,128)(2,1)}, u32[]{:S(2)}) copy-start(bf16[384,128]{1,0:T(8,128)(2,1)} %constant.12.clone.along_x) | copy-start | bytes 294916
  14.0 0.8 %copy-start.11 = (bf16[128,256]{1,0:T(8,128)(2,1)S(1)}, bf16[128,256]{1,0:T(8,128)(2,1)}, u32[]{:S(2)}) copy-start(bf16[128,256]{1,0:T(8,128)(2,1)} %constant.16.clone.up_x) | copy-start | bytes 196612

commit v2 on v1

--- a/solution.py
+++ b/solution.py
@@ -17,6 +17,7 @@
 FPS = 16
 FY = 64
 FX = 128
+VMEM_BYTES = 60 * 2**20
 PARTS = 4
 
 C = (-205.0 / 72.0, 8.0 / 5.0, -1.0 / 5.0, 8.0 / 315.0, -1.0 / 560.0)
@@ -78,16 +79,16 @@
 def kernel(
     n,
     latent,
-    w1,
-    w2,
+    w1_hbm,
+    w2_hbm,
     head,
-    wavelet,
-    sources,
-    receivers,
-    along_x,
-    along_y,
-    up_x,
-    up_xt,
+    wavelet_hbm,
+    sources_hbm,
+    receivers_hbm,
+    along_x_hbm,
+    along_y_hbm,
+    up_x_hbm,
+    up_xt_hbm,
     prev_hbm,
     cur_hbm,
     adj_hbm,
@@ -96,6 +97,17 @@
     final_out,
     traces_out,
     gradient_out,
+    w1,
+    w2,
+    wavelet,
+    sources,
+    receivers,
+    along_x,
+    along_y,
+    up_x,
+    up_xt,
+    lap0,
+    head_col,
     a1,
     a2,
     wp1,
@@ -137,18 +149,28 @@
     slabs = n // SHOTS
     has_low = slab > 0
     has_high = slab < slabs - 1
-    steps_here = range(STEPS)
 
     inner = pl.ds(4, FPS)
+    pairs = (
+        (latent, a1.at[1]),
+        (w1_hbm, w1),
+        (cur_hbm, field.at[1, inner]),
+        (w2_hbm, w2),
+        (receivers_hbm, receivers),
+        (along_y_hbm, along_y),
+        (along_x_hbm, along_x),
+        (adj_hbm, adj),
+        (up_x_hbm, up_x),
+        (up_zy_hbm, up_zy),
+        (wavelet_hbm, wavelet),
+        (sources_hbm, sources),
+        (prev_hbm, field.at[0, inner]),
+        (up_zyt_hbm, up_zyt),
+        (up_xt_hbm, up_xt),
+    )
     loads = [
-        pltpu.make_async_copy(cur_hbm, field.at[1, inner], local_sem.at[0]),
-        pltpu.make_async_copy(prev_hbm, field.at[0, inner], local_sem.at[1]),
-        pltpu.make_async_copy(up_zy_hbm, up_zy, local_sem.at[2]),
-        pltpu.make_async_copy(adj_hbm, adj, local_sem.at[3]),
-        pltpu.make_async_copy(up_zyt_hbm, up_zyt, local_sem.at[4]),
+        pltpu.make_async_copy(src, dst, local_sem.at[i]) for i, (src, dst) in enumerate(pairs)
     ]
-    for load in loads:
-        load.start()
 
     def remote(src, dst, send, recv, target):
         return pltpu.make_async_remote_copy(
@@ -172,6 +194,8 @@
         return carry
 
     lax.fori_loop(1, n, greet, 0)
+    for load in loads:
+        load.start()
 
     for a in (a1, a2):
 
@@ -183,7 +207,6 @@
         def _():
             a[2] = jnp.zeros((CH, CELLS), BF16)
 
-    a1[1] = latent[...]
     pl.semaphore_wait(barrier, n - 1)
 
     width = CELLS // PARTS
@@ -231,12 +254,14 @@
             def _():
                 lat_copy(side, part).start()
 
+    loads[1].wait()
+    loads[3].wait()
     for w, packed in ((w1, wp1), (w2, wp2)):
         for tap in range(9):
             for dz in range(3):
                 packed[tap * CH : (tap + 1) * CH, dz * CH : (dz + 1) * CH] = w[dz * 9 + tap]
 
-    loads[0].wait()
+    loads[2].wait()
     rim_out[0, 0] = field[1, FPS : FPS + 4].reshape(4 * FY, FX).astype(BF16)
     rim_out[1, 0] = field[1, 4:8].reshape(4 * FY, FX).astype(BF16)
     for side in range(2):
@@ -253,8 +278,8 @@
     def _():
         field[:, FPS + 4 :] = jnp.zeros((2, 4, FY, FX), F32)
 
-    corr[...] = jnp.zeros((FPS * FY, FX), F32)
-    station = receivers[shot]
+    loads[4].wait()
+    station = receivers[:, shot]
     station_row = (station[0:1] - slab * FPS) * FY + station[1:2]
     station_col = station[2:3]
     hot[...] = (
@@ -264,6 +289,15 @@
     )
     col_hot = (lax.broadcasted_iota(jnp.int32, (FX, FX), 0) == station_col).astype(F32)
     rec[...] = jnp.zeros((8, FX), F32)
+
+    square = (CH, CH)
+    diagonal = lax.broadcasted_iota(jnp.int32, square, 0) == lax.broadcasted_iota(
+        jnp.int32, square, 1
+    )
+    spread = jnp.broadcast_to(head[...].astype(F32), square)
+    head_col[...] = jnp.broadcast_to(
+        jnp.sum(jnp.where(diagonal, spread, 0.0), axis=1, keepdims=True), (CH, 128)
+    )
 
     cell = lax.broadcasted_iota(jnp.int32, (1, CELLS), 1)
     col = lax.rem(cell, CX)
@@ -295,6 +329,7 @@
         )
         return jnp.where(v > 0, v, LEAK * v)
 
+    loads[0].wait()
     for part in range(PARTS):
         for side in range(2):
 
@@ -317,6 +352,77 @@
         return carry
 
     lax.fori_loop(0, PARTS, hidden_part, 0)
+    def laplace(cur, chunks):
+        centres = [field[cur, 4 + 4 * c : 8 + 4 * c].reshape(4 * FY, FX) for c in chunks]
+        halves = [two(v) for v in centres]
+        across = jnp.concatenate(
+            [jnp.concatenate([hi, lo, hi], axis=0) for hi, lo in halves], axis=1
+        )
+        from_rows = dot(along_y[...], across)
+        laps = []
+        for i, c in enumerate(chunks):
+            hi, lo = halves[i]
+            lap = from_rows[:, FX * i : FX * (i + 1)]
+            lap = lap + dot(jnp.concatenate([hi, lo, hi], axis=1), along_x[...])
+            lap = lap + C[0] * centres[i]
+            at = 4 + 4 * c
+            for k in range(1, 5):
+                near = field[cur, at - k : at - k + 4] + field[cur, at + k : at + k + 4]
+                lap = lap + C[k] * near.reshape(4 * FY, FX)
+            laps.append(lap)
+        return laps
+
+    def advance(t, cur, old, c, lap):
+        at = 4 + 4 * c
+        courant = COURANT * speed[4 * FY * c : 4 * FY * (c + 1)]
+        pulse = jnp.where(linear == source_at - c * 4 * FY * FX, wavelet[t, shot], 0.0)
+        v = field[cur, at : at + 4].reshape(4 * FY, FX)
+        before = field[old, at : at + 4].reshape(4 * FY, FX)
+        new = 2.0 * v - before + courant * courant * lap + pulse
+        field[old, at : at + 4] = new.reshape(4, FY, FX)
+
+    def weighted(t, c, lap):
+        return adj[t, 4 * c : 4 * c + 4].reshape(4 * FY, FX).astype(F32) * lap
+
+    def take_rims(t, cur):
+        for side in range(2):
+
+            @pl.when(rim_gets[side])
+            def _():
+                rim_copy(side, t).wait_recv()
+                at = (FPS + 4) * side
+                field[cur, at : at + 4] = rim_in[side, t].reshape(4, FY, FX).astype(F32)
+
+    def give_rims(t, old):
+        rim_out[0, t + 1] = field[old, FPS : FPS + 4].reshape(4 * FY, FX).astype(BF16)
+        rim_out[1, t + 1] = field[old, 4:8].reshape(4 * FY, FX).astype(BF16)
+        for side in range(2):
+
+            @pl.when(rim_sends[side])
+            def _():
+                rim_copy(side, t + 1).start()
+
+    def record(t, old):
+        hi, lo = two(field[old, 4 : 4 + FPS].reshape(FPS * FY, FX))
+        seen = dot(hi, hot[...], ((0,), (0,))) + dot(lo, hot[...], ((0,), (0,)))
+        seen = jnp.sum(seen * col_hot, axis=0, keepdims=True)
+        rec[...] += jnp.where(lax.broadcasted_iota(jnp.int32, (8, FX), 0) == t, seen, 0.0)
+
+    for i in (5, 6, 7, 8, 9, 10, 11, 12):
+        loads[i].wait()
+    source_at = (
+        (sources[0, shot] - slab * FPS) * (FY * FX) + sources[1, shot] * FX + sources[2, shot]
+    )
+    linear = lax.broadcasted_iota(jnp.int32, (4 * FY, FX), 0) * FX + lax.broadcasted_iota(
+        jnp.int32, (4 * FY, FX), 1
+    )
+
+    take_rims(0, 1)
+    for chunks in ((0, 3), (1, 2)):
+        for c, lap in zip(chunks, laplace(1, chunks)):
+            rows = slice(4 * FY * c, 4 * FY * (c + 1))
+            lap0[rows] = lap
+            corr[rows] = weighted(0, c, lap)
     for part in range(PARTS):
         for side in range(2):
 
@@ -329,7 +435,7 @@
 
     def logit_part(part, acc):
         first = pl.multiple_of(part * 8, 8)
-        return acc + head[pl.ds(first, 8), 0:1] * gathered(first)
+        return acc + head_col[pl.ds(first, 8), 0:1] * gathered(first)
 
     logits = jnp.sum(
         lax.fori_loop(0, CH // 8, logit_part, jnp.zeros((8, CELLS), F32)), axis=0, keepdims=True
@@ -364,79 +470,38 @@
     wide = dot(jnp.concatenate(planes, axis=0), up_x[...])
     tall = jnp.concatenate([wide[:, :FX], wide[:, FX:]], axis=0)
     hi, lo = two(tall)
-    loads[2].wait()
     speed[...] = dot(up_zy[...], hi) + dot(up_zy[...], lo)
-
-    loads[1].wait()
-    loads[3].wait()
-    source_at = (
-        (sources[shot, 0] - slab * FPS) * (FY * FX) + sources[shot, 1] * FX + sources[shot, 2]
-    )
-    linear = lax.broadcasted_iota(jnp.int32, (4 * FY, FX), 0) * FX + lax.broadcasted_iota(
-        jnp.int32, (4 * FY, FX), 1
-    )
-
-    def pair(t, cur, old, chunks):
-        centres = [field[cur, 4 + 4 * c : 8 + 4 * c].reshape(4 * FY, FX) for c in chunks]
-        halves = [two(v) for v in centres]
-        across = jnp.concatenate(
-            [jnp.concatenate([hi, lo, hi], axis=0) for hi, lo in halves], axis=1
-        )
-        from_rows = dot(along_y[...], across)
-        for i, c in enumerate(chunks):
-            v = centres[i]
-            hi, lo = halves[i]
-            lap = from_rows[:, FX * i : FX * (i + 1)]
-            lap = lap + dot(jnp.concatenate([hi, lo, hi], axis=1), along_x[...])
-            lap = lap + C[0] * v
-            at = 4 + 4 * c
-            for k in range(1, 5):
-                near = field[cur, at - k : at - k + 4] + field[cur, at + k : at + k + 4]
-                lap = lap + C[k] * near.reshape(4 * FY, FX)
-            rows = slice(4 * FY * c, 4 * FY * (c + 1))
-            courant = COURANT * speed[rows]
-            pulse = jnp.where(linear == source_at - c * 4 * FY * FX, wavelet[shot, t], 0.0)
-            before = field[old, at : at + 4].reshape(4 * FY, FX)
-            new = 2.0 * v - before + courant * courant * lap + pulse
-            corr[rows] += adj[t, 4 * c : 4 * c + 4].reshape(4 * FY, FX).astype(F32) * lap
-            field[old, at : at + 4] = new.reshape(4, FY, FX)
 
     def step(t, carry):
         cur = lax.rem(t + 1, 2)
         old = lax.rem(t, 2)
-        for side in range(2):
-
-            @pl.when(rim_gets[side])
-            def _():
-                rim_copy(side, t).wait_recv()
-                at = (FPS + 4) * side
-                field[cur, at : at + 4] = rim_in[side, t].reshape(4, FY, FX).astype(F32)
-
-        pair(t, cur, old, (0, 3))
-
-        @pl.when(t < STEPS - 1)
-        def _():
-            rim_out[0, t + 1] = field[old, FPS : FPS + 4].reshape(4 * FY, FX).astype(BF16)
-            rim_out[1, t + 1] = field[old, 4:8].reshape(4 * FY, FX).astype(BF16)
-            for side in range(2):
-
-                @pl.when(rim_sends[side])
-                def _():
-                    rim_copy(side, t + 1).start()
-
-        pair(t, cur, old, (1, 2))
-        hi, lo = two(field[old, 4 : 4 + FPS].reshape(FPS * FY, FX))
-        seen = dot(hi, hot[...], ((0,), (0,))) + dot(lo, hot[...], ((0,), (0,)))
-        seen = jnp.sum(seen * col_hot, axis=0, keepdims=True)
-        rec[...] += jnp.where(lax.broadcasted_iota(jnp.int32, (8, FX), 0) == t, seen, 0.0)
+        take_rims(t, cur)
+        for chunks in ((0, 3), (1, 2)):
+            for c, lap in zip(chunks, laplace(cur, chunks)):
+                advance(t, cur, old, c, lap)
+                corr[4 * FY * c : 4 * FY * (c + 1)] += weighted(t, c, lap)
+            if chunks[0] == 0:
+                pl.when(t < STEPS - 1)(lambda: give_rims(t, old))
+        record(t, old)
         return carry
 
-    lax.fori_loop(0, STEPS, step, 0)
+    for chunks in ((0, 3), (1, 2)):
+        for c in chunks:
+            advance(0, 1, 0, c, lap0[4 * FY * c : 4 * FY * (c + 1)])
+        if chunks[0] == 0:
+            give_rims(0, 0)
+    record(0, 0)
+    lax.fori_loop(1, STEPS, step, 0)
+    store = pltpu.make_async_copy(
+        field.at[(STEPS + 1) % 2, inner], final_out, local_sem.at[len(pairs)]
+    )
+    store.start()
     over_peers(lambda j: rec_copy(j).start())
 
     fine = (2.0 * COURANT * COURANT) * speed[...] * corr[...]
     hi, lo = two(fine)
-    loads[4].wait()
+    loads[13].wait()
+    loads[14].wait()
     tall = dot(up_zyt[...], hi) + dot(up_zyt[...], lo)
     half = tall.shape[0] // 2
     hi, lo = two(jnp.concatenate([tall[:half], tall[half:]], axis=1))
@@ -482,7 +547,6 @@
     for j in range(1, SHOTS):
         gr_copy(j).start()
 
-    final_out[...] = field[(STEPS + 1) % 2, 4 : 4 + FPS]
 
     recs[0] = rec[...]
     over_peers(lambda j: rec_copy(j).wait_recv())
@@ -513,6 +577,7 @@
 
     gradient_out[...] = total[...]
 
+    store.wait()
     for part in range(PARTS):
         for side in range(2):
 
@@ -521,7 +586,7 @@
                 lat_copy(side, part).wait_send()
                 hid_copy(side, part).wait_send()
 
-    for t in steps_here:
+    for t in range(STEPS):
         for side in range(2):
 
             @pl.when(rim_sends[side])
@@ -557,7 +622,6 @@
 ):
     along_x, along_y, up_zy, up_zyt, up_x, up_xt = constants()
     vmem = pl.BlockSpec(memory_space=pltpu.VMEM)
-    smem = pl.BlockSpec(memory_space=pltpu.SMEM)
     hbm = pl.BlockSpec(memory_space=pl.ANY)
     dma = pltpu.SemaphoreType.DMA
     final, traces, gradient = pl.pallas_call(
@@ -567,9 +631,20 @@
             jax.ShapeDtypeStruct((SHOTS, STEPS, 128), F32),
             jax.ShapeDtypeStruct((16, FX), F32),
         ),
-        in_specs=[vmem] * 4 + [smem] * 2 + [vmem] * 5 + [hbm] * 5,
-        out_specs=(vmem, vmem, vmem),
+        in_specs=[hbm] * 3 + [vmem] + [hbm] * 12,
+        out_specs=(hbm, vmem, vmem),
         scratch_shapes=[
+            pltpu.VMEM(conv1_weight.shape, BF16),
+            pltpu.VMEM(conv2_weight.shape, BF16),
+            pltpu.SMEM((STEPS, SHOTS), F32),
+            pltpu.SMEM((3, SHOTS), jnp.int32),
+            pltpu.VMEM((3, SHOTS, 128), jnp.int32),
+            pltpu.VMEM(along_x.shape, BF16),
+            pltpu.VMEM(along_y.shape, BF16),
+            pltpu.VMEM(up_x.shape, BF16),
+            pltpu.VMEM(up_xt.shape, BF16),
+            pltpu.VMEM((FPS * FY, FX), F32),
+            pltpu.VMEM((CH, 128), F32),
             pltpu.VMEM((3, CH, CELLS), BF16),
             pltpu.VMEM((3, CH, CELLS), BF16),
             pltpu.VMEM((9 * CH, 3 * CH), BF16),
@@ -591,7 +666,7 @@
             pltpu.VMEM((SHOTS + 2, 16, FX), F32),
             pltpu.VMEM((3 * SHOTS, 16, FX), F32),
             pltpu.VMEM((16, FX), F32),
-            dma((5,)),
+            dma((16,)),
             dma((2, PARTS)),
             dma((2, PARTS)),
             dma((2, PARTS)),
@@ -606,16 +681,16 @@
             dma((3 * SHOTS,)),
         ],
         compiler_params=pltpu.CompilerParams(
-            collective_id=0, has_side_effects=True, vmem_limit_bytes=48 * 2**20
+            collective_id=0, has_side_effects=True, vmem_limit_bytes=VMEM_BYTES
         ),
     )(
         latent.reshape(CH, CELLS),
         conv1_weight,
         conv2_weight,
-        jnp.broadcast_to(head.astype(F32)[:, None], (CH, 128)),
-        wavelet,
-        sources,
-        receivers,
+        head.reshape(1, CH),
+        wavelet.T,
+        sources.T,
+        receivers.transpose(1, 0, 2),
         along_x,
         along_y,
         up_x,

time: 69.3 us -> 55.2 us (0.80)
  local copies, waits for them, and re-layouts: 16.2 us -> 3.2 us
    unnamed x30 -> x7, local copies, waits for them, and re-layouts: 15.5 us -> 3.2 us
    broadcast_in_dim x1 -> x0, local copies, waits for them, and re-layouts: 0.73 us -> none  [body(): jnp.broadcast_to(head.astype(F32)[:, None], (CH, 128))]
where the time goes in v2:
time: 55.2 us; the launch traced here: 55 us
  Pallas kernels  51.2 us (93%)
  local copies, waits for them, and re-layouts  3.2 us (6%)
  between operations  0.65 us (1%)
    pallas_call x1, Pallas kernels, body(): pl.pallas_call(functools.partial(kernel, n), out_shape=(jax.ShapeDtypeStr...  51.2 us
    unnamed x7, local copies, waits for them, and re-layouts  3.2 us

profile of v2, /device:TPU:0, one launch (start us, length us, event | category | flops | bytes accessed | tf_op | source)
XLA Modules:
  0.0 55.0 jit_solution(13915265371542214089)
XLA Ops:
  0.6 51.2 %shard_map.175 = (f32[16,64,128]{2,1,0:T(8,128)}, f32[8,4,128]{2,1,0:T(4,128)}, f32[16,128]{1,0:T(8,128)}) custom-call(bf16[64,2048]{1,0:T(8,128)(2,1)} %bitcast.14, bf16[27,64,64]{2,1,0:T(8,128)(2,1)} %w1_hbm.1, bf16[27,64,64]{2,1,0:T(8,128)(2,1)} %w2_hbm.1, bf16[1,64]{1,0:T(2,128)(2,1)} %bitcast.19, f32[4,8]{1,0:T(4,128)} %bitcast.17, s32[3,8]{1,0:T(4,128)} %bitcast.18, ...), custom_call_target="tpu_custom_call" | custom-call | tf_op jit(solution)/shard_map/pallas_call | solution.py:627
  51.8 0.0 copy-start
  51.8 1.9 %copy.22 = f32[1,16,64,128]{3,2,1,0:T(8,128)} copy(f32[1,16,64,128]{3,2,1,0:T(8,128)} %bitcast.11) | data formatting | bytes 1048576
  53.7 0.0 copy-done
  53.7 0.0 copy-start.1
  53.7 0.6 %copy.23 = f32[8,4,128]{2,1,0:T(4,128)} copy(f32[8,4,128]{2,1,0:T(4,128)S(1)} %copy-done) | data formatting | bytes 32768
  54.3 0.1 copy-done.1
  54.4 0.6 %copy.24 = f32[1,2048]{1,0:T(1,128)} copy(f32[1,2048]{1,0:T(1,128)S(1)} %bitcast.16) | data formatting | bytes 16384
Async XLA Ops:
  51.8 1.9 %copy-start = (f32[8,4,128]{2,1,0:T(4,128)S(1)}, f32[8,4,128]{2,1,0:T(4,128)}, u32[]{:S(2)}) copy-start(f32[8,4,128]{2,1,0:T(4,128)} %get-tuple-element.13) | copy-start | bytes 49156
  53.7 0.7 %copy-start.1 = (f32[16,128]{1,0:T(8,128)S(1)}, f32[16,128]{1,0:T(8,128)}, u32[]{:S(2)}) copy-start(f32[16,128]{1,0:T(8,128)} %get-tuple-element.8) | copy-start | bytes 24580

commit v3 on v2

--- a/solution.py
+++ b/solution.py
@@ -264,12 +264,6 @@
     loads[2].wait()
     rim_out[0, 0] = field[1, FPS : FPS + 4].reshape(4 * FY, FX).astype(BF16)
     rim_out[1, 0] = field[1, 4:8].reshape(4 * FY, FX).astype(BF16)
-    for side in range(2):
-
-        @pl.when(rim_sends[side])
-        def _():
-            rim_copy(side, 0).start()
-
     @pl.when(jnp.logical_not(has_low))
     def _():
         field[:, 0:4] = jnp.zeros((2, 4, FY, FX), F32)
@@ -339,6 +333,12 @@
 
         multiply(wp1, a1, part)
 
+    for side in range(2):
+
+        @pl.when(rim_sends[side])
+        def _():
+            rim_copy(side, 0).start()
+
     def hidden_part(part, carry):
         first = pl.multiple_of(part * height, height)
         pieces = [gathered(pl.multiple_of(first + 8 * h, 8)) for h in range(height // 8)]
@@ -352,7 +352,7 @@
         return carry
 
     lax.fori_loop(0, PARTS, hidden_part, 0)
-    def laplace(cur, chunks):
+    def in_plane(cur, chunks):
         centres = [field[cur, 4 + 4 * c : 8 + 4 * c].reshape(4 * FY, FX) for c in chunks]
         halves = [two(v) for v in centres]
         across = jnp.concatenate(
@@ -364,13 +364,21 @@
             hi, lo = halves[i]
             lap = from_rows[:, FX * i : FX * (i + 1)]
             lap = lap + dot(jnp.concatenate([hi, lo, hi], axis=1), along_x[...])
-            lap = lap + C[0] * centres[i]
+            laps.append(lap + C[0] * centres[i])
+        return laps
+
+    def in_depth(cur, chunks, laps):
+        whole = []
+        for c, lap in zip(chunks, laps):
             at = 4 + 4 * c
             for k in range(1, 5):
                 near = field[cur, at - k : at - k + 4] + field[cur, at + k : at + k + 4]
                 lap = lap + C[k] * near.reshape(4 * FY, FX)
-            laps.append(lap)
-        return laps
+            whole.append(lap)
+        return whole
+
+    def laplace(cur, chunks):
+        return in_depth(cur, chunks, in_plane(cur, chunks))
 
     def advance(t, cur, old, c, lap):
         at = 4 + 4 * c
@@ -475,13 +483,18 @@
     def step(t, carry):
         cur = lax.rem(t + 1, 2)
         old = lax.rem(t, 2)
+        outer, middle = (0, 3), (1, 2)
+        laps = in_plane(cur, outer)
         take_rims(t, cur)
-        for chunks in ((0, 3), (1, 2)):
-            for c, lap in zip(chunks, laplace(cur, chunks)):
-                advance(t, cur, old, c, lap)
-                corr[4 * FY * c : 4 * FY * (c + 1)] += weighted(t, c, lap)
-            if chunks[0] == 0:
-                pl.when(t < STEPS - 1)(lambda: give_rims(t, old))
+        laps = in_depth(cur, outer, laps)
+        for c, lap in zip(outer, laps):
+            advance(t, cur, old, c, lap)
+        pl.when(t < STEPS - 1)(lambda: give_rims(t, old))
+        laps = laps + laplace(cur, middle)
+        for c, lap in zip(middle, laps[2:]):
+            advance(t, cur, old, c, lap)
+        for c, lap in zip(outer + middle, laps):
+            corr[4 * FY * c : 4 * FY * (c + 1)] += weighted(t, c, lap)
         record(t, old)
         return carry
 

time: 55.2 us -> 53.5 us (0.969)
  Pallas kernels: 51.2 us -> 49.5 us
    pallas_call x1, Pallas kernels: 51.2 us -> 49.5 us  [body(): pl.pallas_call(functools.partial(kernel, n), out_shape=(jax.ShapeDtypeStr...]
where the time goes in v3:
time: 53.5 us; the launch traced here: 53.3 us
  Pallas kernels  49.5 us (93%)
  local copies, waits for them, and re-layouts  3.2 us (6%)
  between operations  0.65 us (1%)
    pallas_call x1, Pallas kernels, body(): pl.pallas_call(functools.partial(kernel, n), out_shape=(jax.ShapeDtypeStr...  49.5 us
    unnamed x7, local copies, waits for them, and re-layouts  3.2 us

profile of v3, /device:TPU:0, one launch (start us, length us, event | category | flops | bytes accessed | tf_op | source)
XLA Modules:
  0.0 53.3 jit_solution(7090265917448458558)
XLA Ops:
  0.6 49.5 %shard_map.175 = (f32[16,64,128]{2,1,0:T(8,128)}, f32[8,4,128]{2,1,0:T(4,128)}, f32[16,128]{1,0:T(8,128)}) custom-call(bf16[64,2048]{1,0:T(8,128)(2,1)} %bitcast.14, bf16[27,64,64]{2,1,0:T(8,128)(2,1)} %w1_hbm.1, bf16[27,64,64]{2,1,0:T(8,128)(2,1)} %w2_hbm.1, bf16[1,64]{1,0:T(2,128)(2,1)} %bitcast.19, f32[4,8]{1,0:T(4,128)} %bitcast.17, s32[3,8]{1,0:T(4,128)} %bitcast.18, ...), custom_call_target="tpu_custom_call" | custom-call | tf_op jit(solution)/shard_map/pallas_call | solution.py:640
  50.1 0.0 copy-start
  50.1 1.9 %copy.22 = f32[1,16,64,128]{3,2,1,0:T(8,128)} copy(f32[1,16,64,128]{3,2,1,0:T(8,128)} %bitcast.11) | data formatting | bytes 1048576
  52.0 0.0 copy-done
  52.0 0.0 copy-start.1
  52.0 0.6 %copy.23 = f32[8,4,128]{2,1,0:T(4,128)} copy(f32[8,4,128]{2,1,0:T(4,128)S(1)} %copy-done) | data formatting | bytes 32768
  52.6 0.1 copy-done.1
  52.7 0.6 %copy.24 = f32[1,2048]{1,0:T(1,128)} copy(f32[1,2048]{1,0:T(1,128)S(1)} %bitcast.16) | data formatting | bytes 16384
Async XLA Ops:
  50.1 1.9 %copy-start = (f32[8,4,128]{2,1,0:T(4,128)S(1)}, f32[8,4,128]{2,1,0:T(4,128)}, u32[]{:S(2)}) copy-start(f32[8,4,128]{2,1,0:T(4,128)} %get-tuple-element.13) | copy-start | bytes 49156
  52.0 0.7 %copy-start.1 = (f32[16,128]{1,0:T(8,128)S(1)}, f32[16,128]{1,0:T(8,128)}, u32[]{:S(2)}) copy-start(f32[16,128]{1,0:T(8,128)} %get-tuple-element.8) | copy-start | bytes 24580
